TPU v7x, 32 devices: a whole 2x2x4 slice. The times are simulated.
32 devices in a mesh: ffn: 8 (over z, core), mp: 4 (over y, x).
Axes of the slice: x: 2, y: 2, z: 4, core: 2. Of those that a mesh axis runs over, the one named last changes fastest.
Arguments:
- hidden_in: bfloat16 [256, 8192], P(None, 'mp'), may hold values from -40 to 40
- norm_gain: float32 [8192], P('mp'), may hold values from 0.1 to 1.9
- grad_out: bfloat16 [256, 8192], P(None, 'mp'), may hold values from -6 to 6
- gate_weight: bfloat16 [8192, 28672], P('mp', 'ffn'), may hold values from -0.0625 to 0.0625
- up_weight: bfloat16 [8192, 28672], P('mp', 'ffn'), may hold values from -0.0625 to 0.0625
- down_weight: bfloat16 [28672, 8192], P('ffn', 'mp'), may hold values from -0.03125 to 0.03125
Outputs:
- grad_hidden: bfloat16 [256, 8192], P(None, 'mp')
- grad_gain: float32 [8192], P('mp')
- grad_gate: bfloat16 [8192, 28672], P('mp', 'ffn')
- grad_up: bfloat16 [8192, 28672], P('mp', 'ffn')
- grad_down: bfloat16 [28672, 8192], P('ffn', 'mp')
All inputs are finite; a program needn't handle non-finite values.
Results may differ from a plain program's by a relative error of at most 0.0066.
Values may be sent and summed in bfloat16 or wider, within the bound.
A program may use at most 192 MiB of HBM per device.

v0:
```python
import functools

import jax
import jax.numpy as jnp
from jax import lax
from jax.experimental import pallas as pl
from jax.experimental.pallas import tpu as pltpu
from jax.sharding import PartitionSpec as P

epsilon = 1e-05
F32 = jnp.float32
BF16 = jnp.bfloat16


def swap(x, axis, count, bit):
    return lax.ppermute(x, axis, [(i, i ^ bit) for i in range(count)])


def bits_of(count):
    return [1 << b for b in range(count.bit_length() - 1)]


def relative(x, me, count):
    rows = x.shape[0] // count
    parts = [lax.dynamic_slice_in_dim(x, (me ^ r) * rows, rows, 0) for r in range(count)]
    return jnp.concatenate(parts, axis=0)


def all_sum(x, axis, count):
    for bit in bits_of(count):
        x = x + swap(x, axis, count, bit)
    return x


def pick(x, held, wanted, total):
    rows = total // len(held)
    parts = [x[..., k * rows:(k + 1) * rows, :] for k, r in enumerate(held) if r in wanted]
    return jnp.concatenate(parts, axis=-2)


def scatter_sum(mine, out, axis, count, order, types):
    received = swap(out, axis, count, order[0])
    held = [r for r in range(count) if not r & order[0]]
    return finish_sum(mine, received, held, axis, count, order, types)


def finish_sum(x, received, held, axis, count, order, types):
    for bit, kind in zip(order[1:], types[1:]):
        x = x + received.astype(F32)
        keep = [r for r in held if not r & bit]
        send = [r for r in held if r & bit]
        total = x.shape[-2]
        out = pick(x, held, send, total).astype(kind)
        x = pick(x, held, keep, total)
        received = swap(out, axis, count, bit)
        held = keep
    return x, received


def gather(x, axis, count, order):
    blocks = {0: x}
    for bit in order:
        have = sorted(blocks)
        rows = x.shape[-2]
        got = swap(jnp.concatenate([blocks[r] for r in have], axis=-2), axis, count, bit)
        for k, r in enumerate(have):
            blocks[r ^ bit] = got[..., k * rows:(k + 1) * rows, :]
    return jnp.concatenate([blocks[r] for r in range(count)], axis=-2)


def dot(a, b, da, db):
    return lax.dot_general(a, b, (((da,), (db,)), ((), ())), preferred_element_type=F32)


TILE = 256
LIGHT = pl.CostEstimate(flops=1, bytes_accessed=1, transcendentals=0)


def cuts(width):
    if width % TILE == 0 and width // TILE >= 4:
        units = width // TILE
        return [(units // 4 + (1 if p < units % 4 else 0)) * TILE for p in range(4)]
    return [width - width // 2, width // 2]


def forward_kernel(count, bit, scaled, grad_out, gate, up, down, *rest):
    keep, send = rest[-2:]
    rows = scaled.shape[0] // count
    for k in range(3):
        if k < 2:
            part = dot(scaled[...], (gate, up)[k][...], 1, 0)
        else:
            part = dot(grad_out[...], down[...], 1, 1)
        kept = sent = 0
        for r in range(count):
            block = part[r * rows:(r + 1) * rows]
            if r & bit:
                send[k, sent * rows:(sent + 1) * rows, :] = block.astype(BF16)
                sent += 1
            else:
                keep[k, kept * rows:(kept + 1) * rows, :] = block
                kept += 1


def forward(scaled, grad_out, gate_weight, up_weight, down_weight, first, size, count, bit, after):
    tokens, local = scaled.shape
    base = first // TILE
    whole = pl.BlockSpec((tokens, local), lambda j: (0, 0))
    column = pl.BlockSpec((local, TILE), lambda j: (0, base + j))
    result = pl.BlockSpec((3, tokens // 2, TILE), lambda j: (0, 0, j))
    extra = list(after)
    return pl.pallas_call(
        functools.partial(forward_kernel, count, bit),
        grid=(size // TILE,),
        in_specs=[whole, whole, column, column, pl.BlockSpec((TILE, local), lambda j: (base + j, 0))]
        + [pl.BlockSpec(memory_space=pl.ANY)] * len(extra),
        out_specs=[result, result],
        out_shape=[
            jax.ShapeDtypeStruct((3, tokens // 2, size), F32),
            jax.ShapeDtypeStruct((3, tokens // 2, size), BF16),
        ],
        compiler_params=pltpu.CompilerParams(vmem_limit_bytes=32 * 2**20),
        cost_estimate=LIGHT,
    )(scaled, grad_out, gate_weight, up_weight, down_weight, *extra)


def activation_kernel(mine, received, inverse, *rest):
    out = rest[-1]
    scale = inverse[...]
    gate = scale * (mine[0] + received[0].astype(F32))
    up_val = scale * (mine[1] + received[1].astype(F32))
    act_grad = mine[2] + received[2].astype(F32)
    sigma = 1.0 / (1.0 + jnp.exp(-gate))
    out[0] = (gate * sigma * up_val).astype(BF16)
    out[1] = (scale * act_grad * up_val * sigma * (1.0 + gate * (1.0 - sigma))).astype(BF16)
    out[2] = (scale * act_grad * gate * sigma).astype(BF16)


def activate(mine, received, inverse, after):
    _, rows, size = mine.shape
    block = pl.BlockSpec((3, rows, TILE), lambda j: (0, 0, j))
    extra = [] if after is None else [after]
    return pl.pallas_call(
        activation_kernel,
        grid=(size // TILE,),
        in_specs=[block, block, pl.BlockSpec((rows, 1), lambda j: (0, 0))]
        + [pl.BlockSpec(memory_space=pl.ANY)] * len(extra),
        out_specs=block,
        out_shape=jax.ShapeDtypeStruct(mine.shape, BF16),
        cost_estimate=LIGHT,
    )(mine, received, inverse, *extra)


def transpose_kernel(x, after, out):
    out[...] = x[...].T


def transpose(x, after):
    rows, columns = x.shape
    return pl.pallas_call(
        transpose_kernel,
        grid=(columns // TILE,),
        in_specs=[pl.BlockSpec((rows, TILE), lambda j: (0, j)), pl.BlockSpec(memory_space=pl.ANY)],
        out_specs=pl.BlockSpec((TILE, rows), lambda j: (j, 0)),
        out_shape=jax.ShapeDtypeStruct((columns, rows), x.dtype),
        cost_estimate=LIGHT,
    )(x, after)


def rows_kernel(mine, received, hidden, gain, after, total, products, gain_part):
    value = mine[...] + received[...].astype(F32)
    term = hidden[...].astype(F32) * value
    total[...] = value
    products[...] = jnp.sum(term * gain[...], axis=1, keepdims=True)
    gain_part[...] = jnp.sum(term, axis=0, keepdims=True)


def finish_rows(mine, received, hidden, gain, after):
    rows, columns = mine.shape
    vmem = pl.BlockSpec(memory_space=pltpu.VMEM)
    return pl.pallas_call(
        rows_kernel,
        in_specs=[vmem] * 4 + [pl.BlockSpec(memory_space=pl.ANY)],
        out_specs=[vmem] * 3,
        out_shape=[
            jax.ShapeDtypeStruct((rows, columns), F32),
            jax.ShapeDtypeStruct((rows, 1), F32),
            jax.ShapeDtypeStruct((1, columns), F32),
        ],
        cost_estimate=LIGHT,
    )(mine, received, hidden, gain[None, :], after)


def input_step(full, gate, up, before, total):
    @pl.when(pl.program_id(0) == 0)
    def _():
        total[...] = jnp.zeros_like(total) if before is None else before[...]

    total[...] += dot(full[1], gate[...], 1, 1) + dot(full[2], up[...], 1, 1)


def weight_step(full, scaled_t, grad_out, grad_gate, grad_up, grad_down):
    grad_gate[...] = dot(scaled_t[...], full[1], 1, 0).astype(BF16)
    grad_up[...] = dot(scaled_t[...], full[2], 1, 0).astype(BF16)
    grad_down[...] = dot(full[0], grad_out[...], 0, 0).astype(BF16)


def backward_kernel(with_input, with_weights, has_before, has_grads, *refs):
    refs = list(refs)
    full = refs.pop(0)
    if with_input:
        gate, up = refs.pop(0), refs.pop(0)
        before = refs.pop(0) if has_before else None
    if with_weights:
        scaled_t, grad_out = refs.pop(0), refs.pop(0)
        if has_grads:
            refs = refs[3:]
    if with_input:
        input_step(full, gate, up, before, refs.pop(0))
    if with_weights:
        weight_step(full, scaled_t, grad_out, *refs)


def backward(full, first, weights=None, before=None, tall=None, grads=None, shapes=None):
    size = full.shape[2]
    tokens = full.shape[1]
    base = first // TILE
    local = weights[0].shape[0] if weights is not None else tall[0].shape[0]
    column = pl.BlockSpec((local, TILE), lambda j: (0, base + j))
    row = pl.BlockSpec((TILE, local), lambda j: (base + j, 0))
    whole = pl.BlockSpec((tokens, local), lambda j: (0, 0))
    operands = [full]
    in_specs = [pl.BlockSpec((3, tokens, TILE), lambda j: (0, 0, j))]
    out_specs, out_shape, aliases = [], [], {}
    flops = moved = 0
    if weights is not None:
        operands += list(weights)
        in_specs += [column, column]
        if before is not None:
            operands.append(before)
            in_specs.append(whole)
        out_specs.append(whole)
        out_shape.append(jax.ShapeDtypeStruct((tokens, local), F32))
        flops += 4 * tokens * local * size
        moved += 4 * local * size
    if tall is not None:
        operands += list(tall)
        in_specs += [pl.BlockSpec((local, tokens), lambda j: (0, 0)), whole]
        if grads is not None:
            for k in range(3):
                aliases[len(operands) + k] = len(out_shape) + k
            operands += list(grads)
            in_specs += [pl.BlockSpec(memory_space=pl.ANY)] * 3
        out_specs += [column, column, row]
        out_shape += shapes
        flops += 6 * tokens * local * size
        moved += 6 * local * size
    return pl.pallas_call(
        functools.partial(
            backward_kernel, weights is not None, tall is not None, before is not None, grads is not None
        ),
        grid=(size // TILE,),
        in_specs=in_specs,
        out_specs=out_specs,
        out_shape=out_shape,
        input_output_aliases=aliases,
        compiler_params=pltpu.CompilerParams(vmem_limit_bytes=44 * 2**20),
        cost_estimate=LIGHT if weights is not None else pl.CostEstimate(
            flops=flops, bytes_accessed=moved, transcendentals=0
        ),
    )(*operands)


def build(mp, ffn):
    def body(hidden_in, norm_gain, grad_out, gate_weight, up_weight, down_weight):
        tokens, local = hidden_in.shape
        features = local * mp
        width = gate_weight.shape[1]
        m = lax.axis_index("mp")
        f = lax.axis_index("ffn")
        sizes = cuts(width)
        tiled = all(size % TILE == 0 for size in sizes)
        hidden_r = relative(hidden_in, m, mp)
        grad_out_r = relative(grad_out, m, mp)
        scaled = (hidden_r.astype(F32) * norm_gain).astype(BF16)

        order = bits_of(mp)
        blocks = list(range(mp))
        first = 0
        starts, kept, sent, arrived = [], [], [], []
        for piece, size in enumerate(sizes):
            way = order if piece % 2 == 0 else order[::-1]
            cols = slice(first, first + size)
            starts.append(first)
            if tiled:
                keep, send = forward(
                    scaled, grad_out_r, gate_weight, up_weight, down_weight, first, size, mp, way[0],
                    sent[-1:] + arrived[:-1][-1:],
                )
            else:
                parts = jnp.stack([
                    dot(scaled, gate_weight[:, cols], 1, 0),
                    dot(scaled, up_weight[:, cols], 1, 0),
                    dot(grad_out_r, down_weight[cols, :], 1, 1),
                ])
                keep = pick(parts, blocks, [r for r in blocks if not r & way[0]], tokens)
                send = pick(parts, blocks, [r for r in blocks if r & way[0]], tokens).astype(BF16)
            kept.append(keep)
            sent.append(send)
            arrived.append(swap(send, "mp", mp, way[0]))
            first += size

        late, _ = lax.optimization_barrier((hidden_in, sent[0]))
        hidden = late.astype(F32)
        square_sum = all_sum(jnp.sum(hidden * hidden, axis=1), "mp", mp)
        inverse = lax.rsqrt(square_sum / features + epsilon)
        mp_rows = tokens // mp
        mine_inverse = lax.dynamic_slice_in_dim(inverse, m * mp_rows, mp_rows, 0)[:, None]

        shapes = [
            jax.ShapeDtypeStruct(w.shape, BF16) for w in (gate_weight, up_weight, down_weight)
        ]
        scaled_t = transpose(scaled, sent[1]) if tiled else None
        input_part = grads = None
        finals, totals = [], []
        for piece, size in enumerate(sizes):
            way = order if piece % 2 == 0 else order[::-1]
            mine, received = finish_sum(
                kept[piece], arrived[piece], [r for r in blocks if not r & way[0]],
                "mp", mp, way, [BF16] * len(way),
            )
            if tiled:
                results = activate(mine, received, mine_inverse, totals[piece - 2] if piece >= 2 else None)
            else:
                sums = mine + received.astype(F32)
                gate = mine_inverse * sums[0]
                up_val = mine_inverse * sums[1]
                act_grad = sums[2]
                sigma = jax.nn.sigmoid(gate)
                activation = (gate * sigma * up_val).astype(BF16)
                gate_grad = (
                    mine_inverse * act_grad * up_val * sigma * (1.0 + gate * (1.0 - sigma))
                ).astype(BF16)
                up_grad = (mine_inverse * act_grad * gate * sigma).astype(BF16)
                results = jnp.stack([activation, gate_grad, up_grad])
            full = gather(results, "mp", mp, way[::-1])
            finals.append(full)
            begin = starts[piece]
            cols = slice(begin, begin + size)
            if not tiled:
                term = dot(full[1], gate_weight[:, cols], 1, 1) + dot(full[2], up_weight[:, cols], 1, 1)
                input_part = term if input_part is None else input_part + term
            elif piece + 1 < len(sizes):
                input_part, *grads = backward(
                    full, begin, (gate_weight, up_weight), input_part, (scaled_t, grad_out_r), grads, shapes
                )
                totals.append(grads[0])
            else:
                input_part, = backward(full, begin, (gate_weight, up_weight), input_part)
                grads = backward(
                    full, begin, tall=(scaled_t, grad_out_r), grads=grads, shapes=shapes
                )

        if not tiled:
            activation, gate_grad, up_grad = (
                jnp.concatenate([full[k] for full in finals], axis=1) for k in range(3)
            )
            grads = [
                dot(scaled, gate_grad, 0, 0).astype(BF16),
                dot(scaled, up_grad, 0, 0).astype(BF16),
                dot(activation, grad_out_r, 0, 0).astype(BF16),
            ]
        grad_gate, grad_up, grad_down = grads
        ffn_order = bits_of(ffn)
        ordered = relative(relative(input_part, m, mp), f, ffn)
        places = list(range(ffn))
        kinds = [F32] + [BF16] * (len(ffn_order) - 1)
        mine = pick(ordered, places, [r for r in places if not r & ffn_order[0]], tokens)
        away = pick(ordered, places, [r for r in places if r & ffn_order[0]], tokens)
        mine, received = scatter_sum(mine, away.astype(kinds[0]), "ffn", ffn, ffn_order, kinds)
        row_count = tokens // ffn
        rows_in = lax.dynamic_slice_in_dim(hidden_in, f * row_count, row_count, 0)
        rows_hidden = rows_in.astype(F32)
        if tiled:
            input_grad, product_part, gain_part = finish_rows(mine, received, rows_in, norm_gain, grads[0])
            product_part, gain_part = product_part[:, 0], gain_part[0]
        else:
            input_grad = mine + received.astype(F32)
            product_part = jnp.sum(norm_gain * rows_hidden * input_grad, axis=1)
            gain_part = jnp.sum(rows_hidden * input_grad, axis=0)
        rows_inverse = lax.dynamic_slice_in_dim(inverse, f * row_count, row_count, 0)
        products = all_sum(product_part, "mp", mp)
        rows_out = (
            norm_gain * input_grad
            - rows_hidden * (rows_inverse * rows_inverse * products / features)[:, None]
        ).astype(BF16)
        grad_gain = all_sum(gain_part, "ffn", ffn)
        grad_hidden = relative(gather(rows_out, "ffn", ffn, ffn_order[::-1]), f, ffn)
        return (grad_hidden, grad_gain, grad_gate, grad_up, grad_down)

    return body


def solution(mesh):
    placed = (P(None, "mp"), P("mp"), P(None, "mp"), P("mp", "ffn"), P("mp", "ffn"), P("ffn", "mp"))
    return jax.shard_map(
        build(mesh.shape["mp"], mesh.shape["ffn"]),
        mesh=mesh,
        in_specs=placed,
        out_specs=(P(None, "mp"), P("mp"), P("mp", "ffn"), P("mp", "ffn"), P("ffn", "mp")),
        check_vma=False,
    )
```

profile of v0, /device:TPU:0, one launch (start us, length us, event | category | flops | bytes accessed | tf_op | source)
XLA Modules:
  0.0 243.0 jit_solution(16333618951052055491)
XLA Ops:
  0.7 1.7 constant_dynamic-slice_fusion.16
  3.3 5.2 %copy-done = bf16[2048,3584]{1,0:T(8,128)(2,1)S(1)} copy-done((bf16[2048,3584]{1,0:T(8,128)(2,1)S(1)}, bf16[2048,3584]{1,0:T(8,128)(2,1)}, u32[]{:S(2)}) %copy-start) | copy-done | bytes 14680088
  8.5 6.8 %shard_map.101 = (f32[3,128,1024]{2,1,0:T(8,128)S(1)}, bf16[3,128,1024]{2,1,0:T(8,128)(2,1)S(1)}) custom-call(bf16[256,2048]{1,0:T(8,128)(2,1)S(1)} %multiply_convert_fusion.scaled.x, bf16[256,2048]{1,0:T(8,128)(2,1)S(1)} %pad_maximum_fusion.5.grad_out.refs_4_.refs_5_.refs_2_, bf16[2048,3584]{1,0:T(8,128)(2,1)S(1)} %copy-done, bf16[2048,3584]{1,0:T(8,128)(2,1)} %refs_2_.7, ...), custom_call_target="tpu_custom_call" | custom-call | flops 1 | bytes 1 | tf_op jit(solution)/shard_map/pallas_call | solution.py:112
  15.3 3.0 %collective-permute-start = (bf16[3,128,1024]{2,1,0:T(8,128)(2,1)S(1)}, bf16[3,128,1024]{2,1,0:T(8,128)(2,1)S(1)}, u32[]{:S(2)}, u32[]{:S(2)}) collective-permute-start(bf16[3,128,1024]{2,1,0:T(8,128)(2,1)S(1)} %get-tuple-element.32.rest_0_), channel_id=1, source_target_pairs={{0,1},{1,0},{2,3},{3,2},{4,5},{5,4},{6,7},{7,6},{8,9},{9,8},{10,11... | collective-permute-start | bytes 2359304 | tf_op jit(solution)/shard_map/ppermute | solution.py:16
  18.3 6.5 %shard_map.102 = (f32[3,128,1024]{2,1,0:T(8,128)S(1)}, bf16[3,128,1024]{2,1,0:T(8,128)(2,1)S(1)}) custom-call(bf16[256,2048]{1,0:T(8,128)(2,1)S(1)} %multiply_convert_fusion.scaled.x, bf16[256,2048]{1,0:T(8,128)(2,1)S(1)} %pad_maximum_fusion.5.grad_out.refs_4_.refs_5_.refs_2_, bf16[2048,3584]{1,0:T(8,128)(2,1)S(1)} %copy-done, bf16[2048,3584]{1,0:T(8,128)(2,1)} %refs_2_.7, ...), custom_call_target="tpu_custom_call" | custom-call | flops 1 | bytes 1 | tf_op jit(solution)/shard_map/pallas_call | solution.py:112
  24.9 1.6 collective-permute-start.1
  27.4 8.6 %collective-permute-done.4 = f32[256]{0:T(256)S(1)} collective-permute-done((f32[256]{0:T(256)S(1)}, f32[256]{0:T(256)S(1)}, u32[]{:S(2)}, u32[]{:S(2)}) %collective-permute-start.4) | collective-permute-done | bytes 1056 | tf_op jit(solution)/shard_map/ppermute | solution.py:16
  35.9 1.8 collective-permute-start.5
  37.7 6.4 %collective-permute-done.5 = f32[256]{0:T(256)S(1)} collective-permute-done((f32[256]{0:T(256)S(1)}, f32[256]{0:T(256)S(1)}, u32[]{:S(2)}, u32[]{:S(2)}) %collective-permute-start.5) | collective-permute-done | bytes 1056 | tf_op jit(solution)/shard_map/ppermute | solution.py:16
  45.0 1.5 collective-permute-start.9
  47.3 5.2 %copy-done.1 = bf16[2048,3584]{1,0:T(8,128)(2,1)S(1)} copy-done((bf16[2048,3584]{1,0:T(8,128)(2,1)S(1)}, bf16[2048,3584]{1,0:T(8,128)(2,1)}, u32[]{:S(2)}) %copy-start.1) | copy-done | bytes 14680088
  52.4 1.1 copy-done.7
  53.6 6.1 %shard_map.103 = (f32[3,128,768]{2,1,0:T(8,128)S(1)}, bf16[3,128,768]{2,1,0:T(8,128)(2,1)}) custom-call(bf16[256,2048]{1,0:T(8,128)(2,1)S(1)} %multiply_convert_fusion.scaled.x, bf16[256,2048]{1,0:T(8,128)(2,1)S(1)} %pad_maximum_fusion.5.grad_out.refs_4_.refs_5_.refs_2_, bf16[2048,3584]{1,0:T(8,128)(2,1)S(1)} %copy-done.1, bf16[2048,3584]{1,0:T(8,128)(2,1)} %refs_2_.7, ...), custom_call_target="tpu_custom_call" | custom-call | flops 1 | bytes 1 | tf_op jit(solution)/shard_map/pallas_call | solution.py:112
  60.2 1.8 convert_add_fusion.1
  62.0 1.0 slice.113.mine
  63.9 1.1 collective-permute-start.6
  65.0 3.6 %shard_map.106 = bf16[3,64,1024]{2,1,0:T(8,128)(2,1)} custom-call(f32[3,64,1024]{2,1,0:T(8,128)} %slice.113.mine, bf16[3,64,1024]{2,1,0:T(8,128)(2,1)} %collective-permute-done.9.received, f32[64,1]{1,0:T(8,128)} %copy.26.inverse), custom_call_target="tpu_custom_call" | custom-call | flops 1 | bytes 1 | tf_op jit(solution)/shard_map/pallas_call | solution.py:143
  69.2 5.2 %copy-done.2 = bf16[2048,3584]{1,0:T(8,128)(2,1)S(1)} copy-done((bf16[2048,3584]{1,0:T(8,128)(2,1)S(1)}, bf16[2048,3584]{1,0:T(8,128)(2,1)}, u32[]{:S(2)}) %copy-start.2) | copy-done | bytes 14680088
  74.3 6.1 %shard_map.104 = (f32[3,128,768]{2,1,0:T(8,128)S(1)}, bf16[3,128,768]{2,1,0:T(8,128)(2,1)}) custom-call(bf16[256,2048]{1,0:T(8,128)(2,1)S(1)} %multiply_convert_fusion.scaled.x, bf16[256,2048]{1,0:T(8,128)(2,1)S(1)} %pad_maximum_fusion.5.grad_out.refs_4_.refs_5_.refs_2_, bf16[2048,3584]{1,0:T(8,128)(2,1)S(1)} %copy-done.2, bf16[2048,3584]{1,0:T(8,128)(2,1)} %refs_2_.7, ...), custom_call_target="tpu_custom_call" | custom-call | flops 1 | bytes 1 | tf_op jit(solution)/shard_map/pallas_call | solution.py:112
  81.4 1.4 collective-permute-start.2
  82.8 3.6 %shard_map.105 = bf16[3,64,1024]{2,1,0:T(8,128)(2,1)} custom-call(f32[3,64,1024]{2,1,0:T(8,128)} %slice.111.mine, bf16[3,64,1024]{2,1,0:T(8,128)(2,1)} %collective-permute-done.6.received, f32[64,1]{1,0:T(8,128)} %copy.26.inverse), custom_call_target="tpu_custom_call" | custom-call | flops 1 | bytes 1 | tf_op jit(solution)/shard_map/pallas_call | solution.py:143
  87.3 2.0 pad_maximum_fusion.8
  89.3 1.1 collective-permute-start.11
  90.4 5.5 %shard_map.107.refs_3_.refs_4_.refs_1_ = bf16[2048,256]{1,0:T(8,128)(2,1)} custom-call(bf16[256,2048]{1,0:T(8,128)(2,1)} %copy-done.3, bf16[3,128,1024]{2,1,0:T(8,128)(2,1)} %copy-done.5), custom_call_target="tpu_custom_call" | custom-call | flops 1 | bytes 1 | tf_op jit(solution)/shard_map/pallas_call | solution.py:160
  95.9 1.2 convert_add_fusion.2
  98.7 1.9 pad_maximum_fusion.7
  100.7 1.4 collective-permute-start.8
  102.1 1.2 convert_add_fusion.3
  105.1 6.7 %collective-permute-done.11 = bf16[3,128,1024]{2,1,0:T(8,128)(2,1)} collective-permute-done((bf16[3,128,1024]{2,1,0:T(8,128)(2,1)}, bf16[3,128,1024]{2,1,0:T(8,128)(2,1)}, u32[]{:S(2)}, u32[]{:S(2)}) %collective-permute-start.11) | collective-permute-done | bytes 786464 | tf_op jit(solution)/shard_map/ppermute | solution.py:16
  111.8 1.2 fusion.2
  113.0 1.1 pad_maximum_fusion.2.refs_0_
  114.1 1.2 collective-permute-start.3
  115.3 10.5 %shard_map.108 = (f32[256,2048]{1,0:T(8,128)S(1)}, bf16[2048,3584]{1,0:T(8,128)(2,1)}, bf16[2048,3584]{1,0:T(8,128)(2,1)}, bf16[3584,2048]{1,0:T(8,128)(2,1)}) custom-call(bf16[3,256,1024]{2,1,0:T(8,128)(2,1)S(1)} %pad_maximum_fusion.2.refs_0_, bf16[2048,3584]{1,0:T(8,128)(2,1)} %refs_1_.7, bf16[2048,3584]{1,0:T(8,128)(2,1)} %refs_2_.7, ...), custom_call_target="tpu_custom_call" | custom-call | flops 1 | bytes 1 | tf_op jit(solution)/shard_map/pallas_call | solution.py:258
  125.8 1.3 copy-done.10
  127.9 3.1 %shard_map.111 = bf16[3,64,768]{2,1,0:T(8,128)(2,1)} custom-call(f32[3,64,768]{2,1,0:T(8,128)} %slice.117.mine, bf16[3,64,768]{2,1,0:T(8,128)(2,1)} %copy-done.27, f32[64,1]{1,0:T(8,128)} %copy.26.inverse, bf16[2048,3584]{1,0:T(8,128)(2,1)} %get-tuple-element.41.refs_6_.rest_0_), custom_call_target="tpu_custom_call" | custom-call | flops 1 | bytes 1 | tf_op jit(solution)/shard_map/pallas_call | solution.py:143
  132.7 1.5 pad_maximum_fusion.1.refs_0_
  134.2 10.7 %shard_map.109 = (f32[256,2048]{1,0:T(8,128)S(1)}, bf16[2048,3584]{1,0:T(8,128)(2,1)}, bf16[2048,3584]{1,0:T(8,128)(2,1)}, bf16[3584,2048]{1,0:T(8,128)(2,1)}) custom-call(bf16[3,256,1024]{2,1,0:T(8,128)(2,1)S(1)} %pad_maximum_fusion.1.refs_0_, bf16[2048,3584]{1,0:T(8,128)(2,1)} %refs_1_.7, ...), custom_call_target="tpu_custom_call", output_to_operand_aliasing={{1}: (6, {}), {2}: (7, {}), {3}: (8, {})} | custom-call | flops 1 | bytes 1 | tf_op jit(solution)/shard_map/pallas_call | solution.py:258
  144.9 1.3 copy-done.8
  146.2 3.0 %shard_map.110 = bf16[3,64,768]{2,1,0:T(8,128)(2,1)} custom-call(f32[3,64,768]{2,1,0:T(8,128)} %slice.109.mine, bf16[3,64,768]{2,1,0:T(8,128)(2,1)} %collective-permute-done.3.received, f32[64,1]{1,0:T(8,128)} %copy.26.inverse, bf16[2048,3584]{1,0:T(8,128)(2,1)} %get-tuple-element.44.rest_0_.refs_6_), custom_call_target="tpu_custom_call" | custom-call | flops 1 | bytes 1 | tf_op jit(solution)/shard_map/pallas_call | solution.py:143
  150.1 1.8 pad_maximum_fusion.10
  151.9 1.1 collective-permute-start.17
  153.0 6.3 %collective-permute-done.12 = bf16[3,64,768]{2,1,0:T(8,128)(2,1)S(1)} collective-permute-done((bf16[3,64,768]{2,1,0:T(8,128)(2,1)}, bf16[3,64,768]{2,1,0:T(8,128)(2,1)S(1)}, u32[]{:S(2)}, u32[]{:S(2)}) %collective-permute-start.12) | collective-permute-done | bytes 294944 | tf_op jit(solution)/shard_map/ppermute | solution.py:16
  160.3 1.2 collective-permute-start.13
  161.6 5.6 %collective-permute-done.17 = bf16[3,128,768]{2,1,0:T(8,128)(2,1)} collective-permute-done((bf16[3,128,768]{2,1,0:T(8,128)(2,1)}, bf16[3,128,768]{2,1,0:T(8,128)(2,1)}, u32[]{:S(2)}, u32[]{:S(2)}) %collective-permute-start.17) | collective-permute-done | bytes 589856 | tf_op jit(solution)/shard_map/ppermute | solution.py:16
  167.2 1.1 fusion.3
  168.3 1.0 pad_maximum_fusion.4.refs_0_
  169.4 9.2 %shard_map.112 = (f32[256,2048]{1,0:T(8,128)S(1)}, bf16[2048,3584]{1,0:T(8,128)(2,1)}, bf16[2048,3584]{1,0:T(8,128)(2,1)}, bf16[3584,2048]{1,0:T(8,128)(2,1)}) custom-call(bf16[3,256,768]{2,1,0:T(8,128)(2,1)S(1)} %pad_maximum_fusion.4.refs_0_, bf16[2048,3584]{1,0:T(8,128)(2,1)} %refs_1_.7, ...), custom_call_target="tpu_custom_call", output_to_operand_aliasing={{1}: (6, {}), {2}: (7, {}), {3}: (8, {})} | custom-call | flops 1 | bytes 1 | tf_op jit(solution)/shard_map/pallas_call | solution.py:258
  178.6 1.1 pad_maximum_fusion.3.refs_0_
  179.7 4.8 %shard_map.113 = f32[256,2048]{1,0:T(8,128)S(1)} custom-call(bf16[3,256,768]{2,1,0:T(8,128)(2,1)S(1)} %pad_maximum_fusion.3.refs_0_, bf16[2048,3584]{1,0:T(8,128)(2,1)} %refs_1_.7, bf16[2048,3584]{1,0:T(8,128)(2,1)} %refs_2_.7, f32[256,2048]{1,0:T(8,128)S(1)} %get-tuple-element.49.refs_3_), custom_call_target="tpu_custom_call" | custom-call | flops 1 | bytes 1 | tf_op jit(solution)/shard_map/pallas_call | solution.py:258
  185.5 1.6 constant_dynamic-slice_fusion.hidden
  187.0 1.1 collective-permute-done.18
  188.3 1.6 collective-permute-start.19
  190.0 6.7 %collective-permute-done.19 = bf16[64,2048]{1,0:T(8,128)(2,1)S(1)} collective-permute-done((bf16[64,2048]{1,0:T(8,128)(2,1)S(1)}, bf16[64,2048]{1,0:T(8,128)(2,1)S(1)}, u32[]{:S(2)}, u32[]{:S(2)}) %collective-permute-start.19) | collective-permute-done | bytes 262176 | tf_op jit(solution)/shard_map/ppermute | solution.py:16
  196.8 2.7 %collective-permute-start.20 = (bf16[32,2048]{1,0:T(8,128)(2,1)S(1)}, bf16[32,2048]{1,0:T(8,128)(2,1)S(1)}, u32[]{:S(2)}, u32[]{:S(2)}) collective-permute-start(bf16[32,2048]{1,0:T(8,128)(2,1)S(1)} %slice.148), channel_id=1, source_target_pairs={{0,16},{4,20},{8,24},{12,28},{16,0},{20,4},{24,8},{28,12},{1,17},{... | collective-permute-start | bytes 393224 | tf_op jit(solution)/shard_map/ppermute | solution.py:16
  199.5 4.8 %shard_map.114 = (bf16[2048,3584]{1,0:T(8,128)(2,1)}, bf16[2048,3584]{1,0:T(8,128)(2,1)}, bf16[3584,2048]{1,0:T(8,128)(2,1)}) custom-call(bf16[3,256,768]{2,1,0:T(8,128)(2,1)S(1)} %pad_maximum_fusion.3.refs_0_, bf16[2048,256]{1,0:T(8,128)(2,1)S(1)} %copy-done.4, ...), custom_call_target="tpu_custom_call", output_to_operand_aliasing={{0}: (3, {}), {1}: (4, {}), {2}: (5, {})} | custom-call | flops 2415919104 | bytes 9437184 | tf_op jit(solution)/shard_map/pallas_call | solution.py:258
  206.0 1.8 shard_map.115
  209.5 2.8 %collective-permute-done.21 = f32[32]{0:T(128)S(1)} collective-permute-done((f32[32]{0:T(128)S(1)}, f32[32]{0:T(128)S(1)}, u32[]{:S(2)}, u32[]{:S(2)}) %collective-permute-start.21) | collective-permute-done | bytes 160 | tf_op jit(solution)/shard_map/ppermute | solution.py:16
  213.2 2.6 %collective-permute-done.22 = f32[32]{0:T(128)S(1)} collective-permute-done((f32[32]{0:T(128)S(1)}, f32[32]{0:T(128)S(1)}, u32[]{:S(2)}, u32[]{:S(2)}) %collective-permute-start.22) | collective-permute-done | bytes 160 | tf_op jit(solution)/shard_map/ppermute | solution.py:16
  215.9 1.1 constant_dynamic-update-slice_fusion.3
  217.1 7.3 %collective-permute-done.23 = bf16[32,2048]{1,0:T(8,128)(2,1)S(1)} collective-permute-done((bf16[32,2048]{1,0:T(8,128)(2,1)S(1)}, bf16[32,2048]{1,0:T(8,128)(2,1)S(1)}, u32[]{:S(2)}, u32[]{:S(2)}) %collective-permute-start.23) | collective-permute-done | bytes 131104 | tf_op jit(solution)/shard_map/ppermute | solution.py:16
  224.5 6.4 %collective-permute-done.24 = bf16[64,2048]{1,0:T(8,128)(2,1)S(1)} collective-permute-done((bf16[64,2048]{1,0:T(8,128)(2,1)S(1)}, bf16[64,2048]{1,0:T(8,128)(2,1)S(1)}, u32[]{:S(2)}, u32[]{:S(2)}) %collective-permute-start.24) | collective-permute-done | bytes 262176 | tf_op jit(solution)/shard_map/ppermute | solution.py:16
  231.5 1.4 collective-permute-done.26
  232.9 3.6 %collective-permute-done.27 = f32[2048]{0:T(1024)S(1)} collective-permute-done((f32[2048]{0:T(1024)S(1)}, f32[2048]{0:T(1024)S(1)}, u32[]{:S(2)}, u32[]{:S(2)}) %collective-permute-start.27) | collective-permute-done | bytes 8224 | tf_op jit(solution)/shard_map/ppermute | solution.py:16
  237.1 4.0 %collective-permute-done.28 = f32[2048]{0:T(1024)S(1)} collective-permute-done((f32[2048]{0:T(1024)S(1)}, f32[2048]{0:T(1024)S(1)}, u32[]{:S(2)}, u32[]{:S(2)}) %collective-permute-start.28) | collective-permute-done | bytes 8224 | tf_op jit(solution)/shard_map/ppermute | solution.py:16
  (142 shorter events, 23.9 us)
Async XLA Ops:
  2.3 0.7 copy-start.29
  3.3 5.2 %copy-start = (bf16[2048,3584]{1,0:T(8,128)(2,1)S(1)}, bf16[2048,3584]{1,0:T(8,128)(2,1)}, u32[]{:S(2)}) copy-start(bf16[2048,3584]{1,0:T(8,128)(2,1)} %refs_1_.7) | copy-start | bytes 44040196
  8.5 60.7 %copy-start.3 = (bf16[256,2048]{1,0:T(8,128)(2,1)}, bf16[256,2048]{1,0:T(8,128)(2,1)S(1)}, u32[]{:S(2)}) copy-start(bf16[256,2048]{1,0:T(8,128)(2,1)S(1)} %multiply_convert_fusion.scaled.x) | copy-start | bytes 3145732
  15.3 11.2 %copy-start.16 = (bf16[256,2048]{1,0:T(8,128)(2,1)S(1)}, bf16[256,2048]{1,0:T(8,128)(2,1)}, u32[]{:S(2)}) copy-start(bf16[256,2048]{1,0:T(8,128)(2,1)} %param.6) | copy-start | bytes 3145732
  15.3 28.8 %collective-permute-start = (bf16[3,128,1024]{2,1,0:T(8,128)(2,1)S(1)}, bf16[3,128,1024]{2,1,0:T(8,128)(2,1)S(1)}, u32[]{:S(2)}, u32[]{:S(2)}) collective-permute-start(bf16[3,128,1024]{2,1,0:T(8,128)(2,1)S(1)} %get-tuple-element.32.rest_0_), channel_id=1, source_target_pairs={{0,1},{1,0},{2,3},{3,2},{4,5},{5,4},{6,7},{7,6},{8,9},{9,8},{10,11... | collective-permute-start | bytes 2359304 | tf_op jit(solution)/shard_map/ppermute | solution.py:16
  24.9 19.5 %copy-start.12 = (f32[3,128,1024]{2,1,0:T(8,128)}, f32[3,128,1024]{2,1,0:T(8,128)S(1)}, u32[]{:S(2)}) copy-start(f32[3,128,1024]{2,1,0:T(8,128)S(1)} %get-tuple-element.38) | copy-start | bytes 4718596
  24.9 22.4 %copy-start.5 = (bf16[3,128,1024]{2,1,0:T(8,128)(2,1)}, bf16[3,128,1024]{2,1,0:T(8,128)(2,1)S(1)}, u32[]{:S(2)}) copy-start(bf16[3,128,1024]{2,1,0:T(8,128)(2,1)S(1)} %get-tuple-element.33.rest_0_.after) | copy-start | bytes 2359300
  24.9 35.3 %collective-permute-start.1 = (bf16[3,128,1024]{2,1,0:T(8,128)(2,1)S(1)}, bf16[3,128,1024]{2,1,0:T(8,128)(2,1)}, u32[]{:S(2)}, u32[]{:S(2)}) collective-permute-start(bf16[3,128,1024]{2,1,0:T(8,128)(2,1)S(1)} %get-tuple-element.33.rest_0_.after), channel_id=1, source_target_pairs={{0,2},{1,3},{2,0},{3,1},{4,6},{5,7},{6,4},{7,5},{8,10},{9,11},{10,... | collective-permute-start | bytes 2359304 | tf_op jit(solution)/shard_map/ppermute | solution.py:16
  26.8 9.2 %collective-permute-start.4 = (f32[256]{0:T(256)S(1)}, f32[256]{0:T(256)S(1)}, u32[]{:S(2)}, u32[]{:S(2)}) collective-permute-start(f32[256]{0:T(256)S(1)} %multiply_reduce_fusion), channel_id=1, source_target_pairs={{0,1},{1,0},{2,3},{3,2},{4,5},{5,4},{6,7},{7,6},{8,9},{9,8},{10,11... | collective-permute-start | bytes 3080 | tf_op jit(solution)/shard_map/ppermute | solution.py:16
  35.9 8.1 %collective-permute-start.5 = (f32[256]{0:T(256)S(1)}, f32[256]{0:T(256)S(1)}, u32[]{:S(2)}, u32[]{:S(2)}) collective-permute-start(f32[256]{0:T(256)S(1)} %add.105), channel_id=1, source_target_pairs={{0,2},{1,3},{2,0},{3,1},{4,6},{5,7},{6,4},{7,5},{8,10},{9,11},{10,... | collective-permute-start | bytes 3080 | tf_op jit(solution)/shard_map/ppermute | solution.py:16
  44.1 0.9 copy-start.6
  44.4 2.1 copy-start.17
  45.0 20.0 %collective-permute-start.9 = (bf16[3,64,1024]{2,1,0:T(8,128)(2,1)S(1)}, bf16[3,64,1024]{2,1,0:T(8,128)(2,1)}, u32[]{:S(2)}, u32[]{:S(2)}) collective-permute-start(bf16[3,64,1024]{2,1,0:T(8,128)(2,1)S(1)} %slice.144), channel_id=1, source_target_pairs={{0,2},{1,3},{2,0},{3,1},{4,6},{5,7},{6,4},{7,5},{8,10},{9,11},{10,... | collective-permute-start | bytes 1179656 | tf_op jit(solution)/shard_map/ppermute | solution.py:16
  47.3 5.2 %copy-start.1 = (bf16[2048,3584]{1,0:T(8,128)(2,1)S(1)}, bf16[2048,3584]{1,0:T(8,128)(2,1)}, u32[]{:S(2)}) copy-start(bf16[2048,3584]{1,0:T(8,128)(2,1)} %refs_1_.7) | copy-start | bytes 44040196
  52.4 1.1 copy-start.7
  53.6 6.6 %copy-start.13 = (f32[3,128,1024]{2,1,0:T(8,128)S(1)}, f32[3,128,1024]{2,1,0:T(8,128)}, u32[]{:S(2)}) copy-start(f32[3,128,1024]{2,1,0:T(8,128)} %copy-done.12) | copy-start | bytes 4718596
  59.6 3.4 %copy-start.14 = (f32[3,128,768]{2,1,0:T(8,128)}, f32[3,128,768]{2,1,0:T(8,128)S(1)}, u32[]{:S(2)}) copy-start(f32[3,128,768]{2,1,0:T(8,128)S(1)} %get-tuple-element.45) | copy-start | bytes 3538948
  59.6 2.3 copy-start.18
  59.7 36.3 %collective-permute-start.14 = (bf16[3,128,768]{2,1,0:T(8,128)(2,1)}, bf16[3,128,768]{2,1,0:T(8,128)(2,1)}, u32[]{:S(2)}, u32[]{:S(2)}) collective-permute-start(bf16[3,128,768]{2,1,0:T(8,128)(2,1)} %get-tuple-element.34.rest_0_), channel_id=1, source_target_pairs={{0,1},{1,0},{2,3},{3,2},{4,5},{5,4},{6,7},{7,6},{8,9},{9,8},{10,11... | collective-permute-start | bytes 1769480 | tf_op jit(solution)/shard_map/ppermute | solution.py:16
  62.0 1.9 copy-start.19
  63.9 18.9 %collective-permute-start.6 = (bf16[3,64,1024]{2,1,0:T(8,128)(2,1)}, bf16[3,64,1024]{2,1,0:T(8,128)(2,1)}, u32[]{:S(2)}, u32[]{:S(2)}) collective-permute-start(bf16[3,64,1024]{2,1,0:T(8,128)(2,1)} %slice.145), channel_id=1, source_target_pairs={{0,1},{1,0},{2,3},{3,2},{4,5},{5,4},{6,7},{7,6},{8,9},{9,8},{10,11... | collective-permute-start | bytes 1179656 | tf_op jit(solution)/shard_map/ppermute | solution.py:16
  68.6 18.7 %collective-permute-start.10 = (bf16[3,64,1024]{2,1,0:T(8,128)(2,1)}, bf16[3,64,1024]{2,1,0:T(8,128)(2,1)}, u32[]{:S(2)}, u32[]{:S(2)}) collective-permute-start(bf16[3,64,1024]{2,1,0:T(8,128)(2,1)} %shard_map.106), channel_id=1, source_target_pairs={{0,2},{1,3},{2,0},{3,1},{4,6},{5,7},{6,4},{7,5},{8,10},{9,11},{10,... | collective-permute-start | bytes 1179656 | tf_op jit(solution)/shard_map/ppermute | solution.py:16
  69.2 5.2 %copy-start.2 = (bf16[2048,3584]{1,0:T(8,128)(2,1)S(1)}, bf16[2048,3584]{1,0:T(8,128)(2,1)}, u32[]{:S(2)}) copy-start(bf16[2048,3584]{1,0:T(8,128)(2,1)} %refs_1_.7) | copy-start | bytes 44040196
  74.3 6.1 %copy-start.20 = (f32[3,128,1024]{2,1,0:T(8,128)S(1)}, f32[3,128,1024]{2,1,0:T(8,128)}, u32[]{:S(2)}) copy-start(f32[3,128,1024]{2,1,0:T(8,128)} %copy-done.19) | copy-start | bytes 4718596
  81.4 20.7 %collective-permute-start.2 = (bf16[3,128,768]{2,1,0:T(8,128)(2,1)}, bf16[3,128,768]{2,1,0:T(8,128)(2,1)}, u32[]{:S(2)}, u32[]{:S(2)}) collective-permute-start(bf16[3,128,768]{2,1,0:T(8,128)(2,1)} %get-tuple-element.36), channel_id=1, source_target_pairs={{0,2},{1,3},{2,0},{3,1},{4,6},{5,7},{6,4},{7,5},{8,10},{9,11},{10,... | collective-permute-start | bytes 1769480 | tf_op jit(solution)/shard_map/ppermute | solution.py:16
  86.4 9.5 %copy-start.15 = (f32[3,128,768]{2,1,0:T(8,128)S(1)}, f32[3,128,768]{2,1,0:T(8,128)}, u32[]{:S(2)}) copy-start(f32[3,128,768]{2,1,0:T(8,128)} %copy-done.14) | copy-start | bytes 3538948
  86.4 12.4 %collective-permute-start.7 = (bf16[3,64,1024]{2,1,0:T(8,128)(2,1)}, bf16[3,64,1024]{2,1,0:T(8,128)(2,1)}, u32[]{:S(2)}, u32[]{:S(2)}) collective-permute-start(bf16[3,64,1024]{2,1,0:T(8,128)(2,1)} %shard_map.105), channel_id=1, source_target_pairs={{0,1},{1,0},{2,3},{3,2},{4,5},{5,4},{6,7},{7,6},{8,9},{9,8},{10,11... | collective-permute-start | bytes 1179656 | tf_op jit(solution)/shard_map/ppermute | solution.py:16
  89.3 22.5 %collective-permute-start.11 = (bf16[3,128,1024]{2,1,0:T(8,128)(2,1)}, bf16[3,128,1024]{2,1,0:T(8,128)(2,1)}, u32[]{:S(2)}, u32[]{:S(2)}) collective-permute-start(bf16[3,128,1024]{2,1,0:T(8,128)(2,1)} %pad_maximum_fusion.8), channel_id=1, source_target_pairs={{0,1},{1,0},{2,3},{3,2},{4,5},{5,4},{6,7},{7,6},{8,9},{9,8},{10,11... | collective-permute-start | bytes 2359304 | tf_op jit(solution)/shard_map/ppermute | solution.py:16
  95.9 2.8 %copy-start.23 = (bf16[3,64,1024]{2,1,0:T(8,128)(2,1)S(1)}, bf16[3,64,1024]{2,1,0:T(8,128)(2,1)}, u32[]{:S(2)}) copy-start(bf16[3,64,1024]{2,1,0:T(8,128)(2,1)} %shard_map.105) | copy-start | bytes 1179652
  98.0 29.1 %collective-permute-start.15 = (bf16[3,64,768]{2,1,0:T(8,128)(2,1)S(1)}, bf16[3,64,768]{2,1,0:T(8,128)(2,1)S(1)}, u32[]{:S(2)}, u32[]{:S(2)}) collective-permute-start(bf16[3,64,768]{2,1,0:T(8,128)(2,1)S(1)} %slice.146), channel_id=1, source_target_pairs={{0,2},{1,3},{2,0},{3,1},{4,6},{5,7},{6,4},{7,5},{8,10},{9,11},{10,... | collective-permute-start | bytes 884744 | tf_op jit(solution)/shard_map/ppermute | solution.py:16
  100.7 32.0 %collective-permute-start.8 = (bf16[3,128,1024]{2,1,0:T(8,128)(2,1)}, bf16[3,128,1024]{2,1,0:T(8,128)(2,1)}, u32[]{:S(2)}, u32[]{:S(2)}) collective-permute-start(bf16[3,128,1024]{2,1,0:T(8,128)(2,1)} %pad_maximum_fusion.7), channel_id=1, source_target_pairs={{0,2},{1,3},{2,0},{3,1},{4,6},{5,7},{6,4},{7,5},{8,10},{9,11},{10,... | collective-permute-start | bytes 2359304 | tf_op jit(solution)/shard_map/ppermute | solution.py:16
  102.1 10.9 %copy-start.24 = (bf16[3,64,1024]{2,1,0:T(8,128)(2,1)S(1)}, bf16[3,64,1024]{2,1,0:T(8,128)(2,1)}, u32[]{:S(2)}) copy-start(bf16[3,64,1024]{2,1,0:T(8,128)(2,1)} %shard_map.106) | copy-start | bytes 1179652
  103.3 1.0 copy-start.21
  105.1 10.2 %copy-start.4 = (bf16[2048,256]{1,0:T(8,128)(2,1)S(1)}, bf16[2048,256]{1,0:T(8,128)(2,1)}, u32[]{:S(2)}) copy-start(bf16[2048,256]{1,0:T(8,128)(2,1)} %shard_map.107.refs_3_.refs_4_.refs_1_) | copy-start | bytes 3145732
  114.1 32.0 %collective-permute-start.3 = (bf16[3,64,768]{2,1,0:T(8,128)(2,1)}, bf16[3,64,768]{2,1,0:T(8,128)(2,1)}, u32[]{:S(2)}, u32[]{:S(2)}) collective-permute-start(bf16[3,64,768]{2,1,0:T(8,128)(2,1)} %slice.147), channel_id=1, source_target_pairs={{0,1},{1,0},{2,3},{3,2},{4,5},{5,4},{6,7},{7,6},{8,9},{9,8},{10,11... | collective-permute-start | bytes 884744 | tf_op jit(solution)/shard_map/ppermute | solution.py:16
  125.8 1.3 copy-start.10
  127.2 0.7 copy-start.27
  127.9 3.9 %copy-start.22 = (f32[3,128,768]{2,1,0:T(8,128)S(1)}, f32[3,128,768]{2,1,0:T(8,128)}, u32[]{:S(2)}) copy-start(f32[3,128,768]{2,1,0:T(8,128)} %copy-done.21) | copy-start | bytes 3538948
  130.9 3.2 %copy-start.11 = (f32[256,2048]{1,0:T(8,128)S(1)}, f32[256,2048]{1,0:T(8,128)}, u32[]{:S(2)}) copy-start(f32[256,2048]{1,0:T(8,128)} %copy-done.10) | copy-start | bytes 6291460
  130.9 19.2 %collective-permute-start.16 = (bf16[3,64,768]{2,1,0:T(8,128)(2,1)}, bf16[3,64,768]{2,1,0:T(8,128)(2,1)}, u32[]{:S(2)}, u32[]{:S(2)}) collective-permute-start(bf16[3,64,768]{2,1,0:T(8,128)(2,1)} %shard_map.111), channel_id=1, source_target_pairs={{0,2},{1,3},{2,0},{3,1},{4,6},{5,7},{6,4},{7,5},{8,10},{9,11},{10,... | collective-permute-start | bytes 884744 | tf_op jit(solution)/shard_map/ppermute | solution.py:16
  144.8 1.3 copy-start.8
  146.2 4.0 %copy-start.25 = (bf16[3,64,768]{2,1,0:T(8,128)(2,1)S(1)}, bf16[3,64,768]{2,1,0:T(8,128)(2,1)}, u32[]{:S(2)}) copy-start(bf16[3,64,768]{2,1,0:T(8,128)(2,1)} %shard_map.111) | copy-start | bytes 884740
  149.2 10.2 %collective-permute-start.12 = (bf16[3,64,768]{2,1,0:T(8,128)(2,1)}, bf16[3,64,768]{2,1,0:T(8,128)(2,1)S(1)}, u32[]{:S(2)}, u32[]{:S(2)}) collective-permute-start(bf16[3,64,768]{2,1,0:T(8,128)(2,1)} %shard_map.110), channel_id=1, source_target_pairs={{0,1},{1,0},{2,3},{3,2},{4,5},{5,4},{6,7},{7,6},{8,9},{9,8},{10,11... | collective-permute-start | bytes 884744 | tf_op jit(solution)/shard_map/ppermute | solution.py:16
  151.9 15.3 %collective-permute-start.17 = (bf16[3,128,768]{2,1,0:T(8,128)(2,1)}, bf16[3,128,768]{2,1,0:T(8,128)(2,1)}, u32[]{:S(2)}, u32[]{:S(2)}) collective-permute-start(bf16[3,128,768]{2,1,0:T(8,128)(2,1)} %pad_maximum_fusion.10), channel_id=1, source_target_pairs={{0,1},{1,0},{2,3},{3,2},{4,5},{5,4},{6,7},{7,6},{8,9},{9,8},{10,11... | collective-permute-start | bytes 1769480 | tf_op jit(solution)/shard_map/ppermute | solution.py:16
  160.3 18.2 %collective-permute-start.13 = (bf16[3,128,768]{2,1,0:T(8,128)(2,1)S(1)}, bf16[3,128,768]{2,1,0:T(8,128)(2,1)}, u32[]{:S(2)}, u32[]{:S(2)}) collective-permute-start(bf16[3,128,768]{2,1,0:T(8,128)(2,1)S(1)} %pad_maximum_fusion.9), channel_id=1, source_target_pairs={{0,2},{1,3},{2,0},{3,1},{4,6},{5,7},{6,4},{7,5},{8,10},{9,11},{10,... | collective-permute-start | bytes 1769480 | tf_op jit(solution)/shard_map/ppermute | solution.py:16
  161.6 7.8 %copy-start.9 = (f32[256,2048]{1,0:T(8,128)S(1)}, f32[256,2048]{1,0:T(8,128)}, u32[]{:S(2)}) copy-start(f32[256,2048]{1,0:T(8,128)} %copy-done.8) | copy-start | bytes 6291460
  169.4 9.2 %copy-start.26 = (bf16[3,64,768]{2,1,0:T(8,128)(2,1)S(1)}, bf16[3,64,768]{2,1,0:T(8,128)(2,1)}, u32[]{:S(2)}) copy-start(bf16[3,64,768]{2,1,0:T(8,128)(2,1)} %shard_map.110) | copy-start | bytes 884740
  185.4 2.7 %collective-permute-start.18 = (f32[128,2048]{1,0:T(8,128)S(1)}, f32[128,2048]{1,0:T(8,128)S(1)}, u32[]{:S(2)}, u32[]{:S(2)}) collective-permute-start(f32[128,2048]{1,0:T(8,128)S(1)} %pad_maximum_fusion.6), channel_id=1, source_target_pairs={{0,4},{4,0},{8,12},{12,8},{16,20},{20,16},{24,28},{28,24},{1,5},{5... | collective-permute-start | bytes 3145736 | tf_op jit(solution)/shard_map/ppermute | solution.py:16
  188.3 8.4 %collective-permute-start.19 = (bf16[64,2048]{1,0:T(8,128)(2,1)S(1)}, bf16[64,2048]{1,0:T(8,128)(2,1)S(1)}, u32[]{:S(2)}, u32[]{:S(2)}) collective-permute-start(bf16[64,2048]{1,0:T(8,128)(2,1)S(1)} %pad_maximum_fusion.12), channel_id=1, source_target_pairs={{0,8},{4,12},{8,0},{12,4},{16,24},{20,28},{24,16},{28,20},{1,9},{5... | collective-permute-start | bytes 786440 | tf_op jit(solution)/shard_map/ppermute | solution.py:16
  196.8 8.5 %collective-permute-start.20 = (bf16[32,2048]{1,0:T(8,128)(2,1)S(1)}, bf16[32,2048]{1,0:T(8,128)(2,1)S(1)}, u32[]{:S(2)}, u32[]{:S(2)}) collective-permute-start(bf16[32,2048]{1,0:T(8,128)(2,1)S(1)} %slice.148), channel_id=1, source_target_pairs={{0,16},{4,20},{8,24},{12,28},{16,0},{20,4},{24,8},{28,12},{1,17},{... | collective-permute-start | bytes 393224 | tf_op jit(solution)/shard_map/ppermute | solution.py:16
  205.3 0.6 copy-start.28
  206.0 9.9 %copy-start.30 = (f32[2048]{0:T(1024)S(1)}, f32[2048]{0:T(1024)}, u32[]{:S(2)}) copy-start(f32[2048]{0:T(1024)} %param.7) | copy-start | bytes 24580
  207.8 23.2 %copy-start.32 = (f32[1,2048]{1,0:T(1,128)S(1)}, f32[1,2048]{1,0:T(1,128)}, u32[]{:S(2)}) copy-start(f32[1,2048]{1,0:T(1,128)} %get-tuple-element.56) | copy-start | bytes 24580
  208.6 3.6 %collective-permute-start.21 = (f32[32]{0:T(128)S(1)}, f32[32]{0:T(128)S(1)}, u32[]{:S(2)}, u32[]{:S(2)}) collective-permute-start(f32[32]{0:T(128)S(1)} %reduce), channel_id=1, source_target_pairs={{0,1},{1,0},{2,3},{3,2},{4,5},{5,4},{6,7},{7,6},{8,9},{9,8},{10,11... | collective-permute-start | bytes 392 | tf_op jit(solution)/shard_map/ppermute | solution.py:16
  212.2 3.5 %collective-permute-start.22 = (f32[32]{0:T(128)S(1)}, f32[32]{0:T(128)S(1)}, u32[]{:S(2)}, u32[]{:S(2)}) collective-permute-start(f32[32]{0:T(128)S(1)} %add.122), channel_id=1, source_target_pairs={{0,2},{1,3},{2,0},{3,1},{4,6},{5,7},{6,4},{7,5},{8,10},{9,11},{10,... | collective-permute-start | bytes 392 | tf_op jit(solution)/shard_map/ppermute | solution.py:16
  217.0 7.4 %collective-permute-start.23 = (bf16[32,2048]{1,0:T(8,128)(2,1)S(1)}, bf16[32,2048]{1,0:T(8,128)(2,1)S(1)}, u32[]{:S(2)}, u32[]{:S(2)}) collective-permute-start(bf16[32,2048]{1,0:T(8,128)(2,1)S(1)} %get-tuple-element.60), channel_id=1, source_target_pairs={{0,16},{4,20},{8,24},{12,28},{16,0},{20,4},{24,8},{28,12},{1,17},{... | collective-permute-start | bytes 393224 | tf_op jit(solution)/shard_map/ppermute | solution.py:16
  224.4 6.4 %collective-permute-start.24 = (bf16[64,2048]{1,0:T(8,128)(2,1)S(1)}, bf16[64,2048]{1,0:T(8,128)(2,1)S(1)}, u32[]{:S(2)}, u32[]{:S(2)}) collective-permute-start(bf16[64,2048]{1,0:T(8,128)(2,1)S(1)} %pad_maximum_fusion.13), channel_id=1, source_target_pairs={{0,8},{4,12},{8,0},{12,4},{16,24},{20,28},{24,16},{28,20},{1,9},{5... | collective-permute-start | bytes 786440 | tf_op jit(solution)/shard_map/ppermute | solution.py:16
  230.9 10.8 %collective-permute-start.25 = (bf16[128,2048]{1,0:T(8,128)(2,1)S(1)}, bf16[128,2048]{1,0:T(8,128)(2,1)S(1)}, u32[]{:S(2)}, u32[]{:S(2)}) collective-permute-start(bf16[128,2048]{1,0:T(8,128)(2,1)S(1)} %pad_maximum_fusion.11), channel_id=1, source_target_pairs={{0,4},{4,0},{8,12},{12,8},{16,20},{20,16},{24,28},{28,24},{1,5},{5... | collective-permute-start | bytes 1572872 | tf_op jit(solution)/shard_map/ppermute | solution.py:16
  231.0 1.9 collective-permute-start.26
  232.9 3.7 %collective-permute-start.27 = (f32[2048]{0:T(1024)S(1)}, f32[2048]{0:T(1024)S(1)}, u32[]{:S(2)}, u32[]{:S(2)}) collective-permute-start(f32[2048]{0:T(1024)S(1)} %add.124), channel_id=1, source_target_pairs={{0,8},{4,12},{8,0},{12,4},{16,24},{20,28},{24,16},{28,20},{1,9},{5... | collective-permute-start | bytes 24584 | tf_op jit(solution)/shard_map/ppermute | solution.py:16
  236.6 4.5 %collective-permute-start.28 = (f32[2048]{0:T(1024)S(1)}, f32[2048]{0:T(1024)S(1)}, u32[]{:S(2)}, u32[]{:S(2)}) collective-permute-start(f32[2048]{0:T(1024)S(1)} %add.125), channel_id=1, source_target_pairs={{0,16},{4,20},{8,24},{12,28},{16,0},{20,4},{24,8},{28,12},{1,17},{... | collective-permute-start | bytes 24584 | tf_op jit(solution)/shard_map/ppermute | solution.py:16
  242.1 1.0 copy-start.31
where the time goes:
time: 245 us; the launch traced here: 243 us
  Pallas kernels  86 us (35%)
  waiting for transfers between devices  69.8 us (28%)
  local copies, waits for them, and re-layouts  36.9 us (15%)
  starting transfers between devices  29.1 us (12%)
  other arithmetic  20 us (8%)
    ppermute x29, waiting for transfers between devices, swap(): return lax.ppermute(x, axis, [(i, i ^ bit) for i in range(count)])  69.8 us
    pallas_call x5, Pallas kernels, backward(): pl.pallas_call(functools.partial(backward_kernel, weights is not None, ta...  40 us
    ppermute x29, starting transfers between devices, swap(): return lax.ppermute(x, axis, [(i, i ^ bit) for i in range(count)])  29.1 us
    pallas_call x4, Pallas kernels, forward(): pl.pallas_call(functools.partial(forward_kernel, count, bit), grid=(size...  25.5 us
    unnamed x79, local copies, waits for them, and re-layouts  24 us
    pallas_call x4, Pallas kernels, activate(): pl.pallas_call(activation_kernel, grid=(size // TILE,), in_specs=[block,...  13.2 us
    concatenate x6, other arithmetic, gather(): jnp.concatenate([blocks[r] for r in have], axis=-2)  6.85 us
    slice x12, local copies, waits for them, and re-layouts, pick(): x[..., k * rows:(k + 1) * rows, :]  6.14 us
  transfers between devices with their start and end apart: 29, of which 15 were waited for; matrix products, arithmetic and copies ran while one was open for 11% of the time, Pallas kernels for 30%

commit v1 on v0

--- a/solution.py
+++ b/solution.py
@@ -119,7 +119,7 @@
             jax.ShapeDtypeStruct((3, tokens // 2, size), F32),
             jax.ShapeDtypeStruct((3, tokens // 2, size), BF16),
         ],
-        compiler_params=pltpu.CompilerParams(vmem_limit_bytes=32 * 2**20),
+        compiler_params=pltpu.CompilerParams(vmem_limit_bytes=51 * 2**20),
         cost_estimate=LIGHT,
     )(scaled, grad_out, gate_weight, up_weight, down_weight, *extra)
 
@@ -189,6 +189,21 @@
         ],
         cost_estimate=LIGHT,
     )(mine, received, hidden, gain[None, :], after)
+
+
+def grad_rows_kernel(value, hidden, factor, gain, after, out):
+    out[...] = (gain[...] * value[...] - hidden[...].astype(F32) * factor[...]).astype(BF16)
+
+
+def grad_rows(value, hidden, factor, gain, after):
+    vmem = pl.BlockSpec(memory_space=pltpu.VMEM)
+    return pl.pallas_call(
+        grad_rows_kernel,
+        in_specs=[vmem] * 4 + [pl.BlockSpec(memory_space=pl.ANY)],
+        out_specs=vmem,
+        out_shape=jax.ShapeDtypeStruct(value.shape, BF16),
+        cost_estimate=LIGHT,
+    )(value, hidden, factor[:, None], gain[None, :], after)
 
 
 def input_step(full, gate, up, before, total):
@@ -264,7 +279,7 @@
         out_specs=out_specs,
         out_shape=out_shape,
         input_output_aliases=aliases,
-        compiler_params=pltpu.CompilerParams(vmem_limit_bytes=44 * 2**20),
+        compiler_params=pltpu.CompilerParams(vmem_limit_bytes=51 * 2**20),
         cost_estimate=LIGHT if weights is not None else pl.CostEstimate(
             flops=flops, bytes_accessed=moved, transcendentals=0
         ),
@@ -284,7 +299,16 @@
         grad_out_r = relative(grad_out, m, mp)
         scaled = (hidden_r.astype(F32) * norm_gain).astype(BF16)
 
+        hidden = hidden_in.astype(F32)
+        square_sum = jnp.sum(hidden * hidden, axis=1)
         order = bits_of(mp)
+        square_sums = []
+        for bit in order:
+            square_sum = square_sum + swap(square_sum, "mp", mp, bit)
+            square_sums.append(square_sum)
+        inverse = lax.rsqrt(square_sum / features + epsilon)
+        mp_rows = tokens // mp
+        mine_inverse = lax.dynamic_slice_in_dim(inverse, m * mp_rows, mp_rows, 0)[:, None]
         blocks = list(range(mp))
         first = 0
         starts, kept, sent, arrived = [], [], [], []
@@ -293,9 +317,17 @@
             cols = slice(first, first + size)
             starts.append(first)
             if tiled:
+                early = []
+                if piece == 0:
+                    early = [square_sums[0][None, :]]
+                elif piece == 1:
+                    early = [mine_inverse]
+                elif piece == 2:
+                    scaled_t = transpose(scaled, sent[1])
+                    early = [scaled_t]
                 keep, send = forward(
                     scaled, grad_out_r, gate_weight, up_weight, down_weight, first, size, mp, way[0],
-                    sent[-1:] + arrived[:-1][-1:],
+                    sent[-1:] + arrived[:-1][-1:] + early,
                 )
             else:
                 parts = jnp.stack([
@@ -310,17 +342,9 @@
             arrived.append(swap(send, "mp", mp, way[0]))
             first += size
 
-        late, _ = lax.optimization_barrier((hidden_in, sent[0]))
-        hidden = late.astype(F32)
-        square_sum = all_sum(jnp.sum(hidden * hidden, axis=1), "mp", mp)
-        inverse = lax.rsqrt(square_sum / features + epsilon)
-        mp_rows = tokens // mp
-        mine_inverse = lax.dynamic_slice_in_dim(inverse, m * mp_rows, mp_rows, 0)[:, None]
-
         shapes = [
             jax.ShapeDtypeStruct(w.shape, BF16) for w in (gate_weight, up_weight, down_weight)
         ]
-        scaled_t = transpose(scaled, sent[1]) if tiled else None
         input_part = grads = None
         finals, totals = [], []
         for piece, size in enumerate(sizes):
@@ -330,7 +354,7 @@
                 "mp", mp, way, [BF16] * len(way),
             )
             if tiled:
-                results = activate(mine, received, mine_inverse, totals[piece - 2] if piece >= 2 else None)
+                results = activate(mine, received, mine_inverse, totals[0] if piece + 1 == len(sizes) else None)
             else:
                 sums = mine + received.astype(F32)
                 gate = mine_inverse * sums[0]
@@ -390,11 +414,15 @@
             gain_part = jnp.sum(rows_hidden * input_grad, axis=0)
         rows_inverse = lax.dynamic_slice_in_dim(inverse, f * row_count, row_count, 0)
         products = all_sum(product_part, "mp", mp)
-        rows_out = (
-            norm_gain * input_grad
-            - rows_hidden * (rows_inverse * rows_inverse * products / features)[:, None]
-        ).astype(BF16)
-        grad_gain = all_sum(gain_part, "ffn", ffn)
+        factor = rows_inverse * rows_inverse * products / features
+        grad_gain = gain_part
+        for bit in ffn_order[:-1]:
+            grad_gain = grad_gain + swap(grad_gain, "ffn", ffn, bit)
+        if tiled:
+            rows_out = grad_rows(input_grad, rows_in, factor, norm_gain, grad_gain[None, :])
+        else:
+            rows_out = (norm_gain * input_grad - rows_hidden * factor[:, None]).astype(BF16)
+        grad_gain = grad_gain + swap(grad_gain, "ffn", ffn, ffn_order[-1])
         grad_hidden = relative(gather(rows_out, "ffn", ffn, ffn_order[::-1]), f, ffn)
         return (grad_hidden, grad_gain, grad_gate, grad_up, grad_down)
 

time: 245 us -> 242 us (0.988)
  Pallas kernels: 86 us -> 104 us
  local copies, waits for them, and re-layouts: 36.9 us -> 19 us
  waiting for transfers between devices: 69.8 us -> 59.3 us
  other arithmetic: 20 us -> 25.6 us
    unnamed x79 -> x74, local copies, waits for them, and re-layouts: 24 us -> 5.66 us
    ppermute x29, waiting for transfers between devices: 69.8 us -> 59.3 us  [swap(): return lax.ppermute(x, axis, [(i, i ^ bit) for i in range(count)])]
    pallas_call x5, Pallas kernels: 40 us -> 49.1 us  [backward(): pl.pallas_call(functools.partial(backward_kernel, weights is not None, ta...]
    pallas_call x4, Pallas kernels: 25.5 us -> 32.6 us  [forward(): pl.pallas_call(functools.partial(forward_kernel, count, bit), grid=(size...]
    concatenate x4, other arithmetic: 4.78 us -> 8.33 us  [gather(): return jnp.concatenate([blocks[r] for r in range(count)], axis=-2)]
  transfers between devices with their start and end apart: 29 -> 29, of which waited for: 15 -> 13; matrix products, arithmetic and copies ran while one was open for 11% -> 13% of each run, Pallas kernels for 30% -> 35%
where the time goes in v1:
time: 242 us; the launch traced here: 240 us
  Pallas kernels  104 us (43%)
  waiting for transfers between devices  59.3 us (25%)
  starting transfers between devices  31.5 us (13%)
  other arithmetic  25.6 us (11%)
  local copies, waits for them, and re-layouts  19 us (8%)
    ppermute x29, waiting for transfers between devices, swap(): return lax.ppermute(x, axis, [(i, i ^ bit) for i in range(count)])  59.3 us
    pallas_call x5, Pallas kernels, backward(): pl.pallas_call(functools.partial(backward_kernel, weights is not None, ta...  49.1 us
    pallas_call x4, Pallas kernels, forward(): pl.pallas_call(functools.partial(forward_kernel, count, bit), grid=(size...  32.6 us
    ppermute x29, starting transfers between devices, swap(): return lax.ppermute(x, axis, [(i, i ^ bit) for i in range(count)])  31.5 us
    pallas_call x4, Pallas kernels, activate(): pl.pallas_call(activation_kernel, grid=(size // TILE,), in_specs=[block,...  13.1 us
    concatenate x4, other arithmetic, gather(): return jnp.concatenate([blocks[r] for r in range(count)], axis=-2)  8.33 us
    concatenate x6, other arithmetic, gather(): jnp.concatenate([blocks[r] for r in have], axis=-2)  7.56 us
    unnamed x74, local copies, waits for them, and re-layouts  5.66 us
  transfers between devices with their start and end apart: 29, of which 13 were waited for; matrix products, arithmetic and copies ran while one was open for 13% of the time, Pallas kernels for 35%

profile of v1, /device:TPU:0, one launch (start us, length us, event | category | flops | bytes accessed | tf_op | source)
XLA Modules:
  0.0 240.4 jit_solution(2345908257890804337)
XLA Ops:
  0.6 1.6 multiply_reduce_fusion
  2.2 3.0 %collective-permute-start = (f32[256]{0:T(256)S(1)}, f32[256]{0:T(256)S(1)}, u32[]{:S(2)}, u32[]{:S(2)}) collective-permute-start(f32[256]{0:T(256)S(1)} %multiply_reduce_fusion), channel_id=1, source_target_pairs={{0,1},{1,0},{2,3},{3,2},{4,5},{5,4},{6,7},{7,6},{8,9},{9,8},{10,11... | collective-permute-start | bytes 3080 | tf_op jit(solution)/shard_map/ppermute | solution.py:16
  5.2 1.3 constant_dynamic-slice_fusion.20
  7.0 8.7 %shard_map.101 = (f32[3,128,1024]{2,1,0:T(8,128)}, bf16[3,128,1024]{2,1,0:T(8,128)(2,1)}) custom-call(bf16[256,2048]{1,0:T(8,128)(2,1)S(1)} %multiply_convert_fusion.scaled.x, bf16[256,2048]{1,0:T(8,128)(2,1)S(1)} %pad_maximum_fusion.5.grad_out.refs_4_.refs_5_.refs_2_, bf16[2048,3584]{1,0:T(8,128)(2,1)} %refs_1_.7, bf16[2048,3584]{1,0:T(8,128)(2,1)} %refs_2_.7, ...), custom_call_target="tpu_custom_call" | custom-call | flops 1 | bytes 1 | tf_op jit(solution)/shard_map/pallas_call | solution.py:112
  15.7 1.2 collective-permute-start.2
  16.9 1.5 collective-permute-start.1
  18.4 2.0 collective-permute-done.1
  20.7 8.7 %shard_map.102 = (f32[3,128,1024]{2,1,0:T(8,128)}, bf16[3,128,1024]{2,1,0:T(8,128)(2,1)S(1)}) custom-call(bf16[256,2048]{1,0:T(8,128)(2,1)S(1)} %multiply_convert_fusion.scaled.x, bf16[256,2048]{1,0:T(8,128)(2,1)} %copy-done, bf16[2048,3584]{1,0:T(8,128)(2,1)} %refs_1_.7, bf16[2048,3584]{1,0:T(8,128)(2,1)} %refs_2_.7, bf16[3584,2048]{1,0:T(8,128)(2,1)} %down.7, ...), custom_call_target="tpu_custom_call" | custom-call | flops 1 | bytes 1 | tf_op jit(solution)/shard_map/pallas_call | solution.py:112
  29.4 1.6 collective-permute-start.3
  30.9 4.0 %collective-permute-done.2.rest_1_ = bf16[3,128,1024]{2,1,0:T(8,128)(2,1)S(1)} collective-permute-done((bf16[3,128,1024]{2,1,0:T(8,128)(2,1)}, bf16[3,128,1024]{2,1,0:T(8,128)(2,1)S(1)}, u32[]{:S(2)}, u32[]{:S(2)}) %collective-permute-start.2) | collective-permute-done | bytes 786464 | tf_op jit(solution)/shard_map/ppermute | solution.py:16
  35.2 1.1 copy-done.9
  36.4 1.6 collective-permute-start.6
  38.0 5.4 %shard_map.103.rest_2_.refs_3_.refs_4_.refs_1_ = bf16[2048,256]{1,0:T(8,128)(2,1)} custom-call(bf16[256,2048]{1,0:T(8,128)(2,1)} %copy-done.3, bf16[3,128,1024]{2,1,0:T(8,128)(2,1)} %copy-done.6), custom_call_target="tpu_custom_call" | custom-call | flops 1 | bytes 1 | tf_op jit(solution)/shard_map/pallas_call | solution.py:160
  43.4 1.1 copy-done.7
  44.5 7.8 %shard_map.104 = (f32[3,128,768]{2,1,0:T(8,128)}, bf16[3,128,768]{2,1,0:T(8,128)(2,1)S(1)}) custom-call(bf16[256,2048]{1,0:T(8,128)(2,1)} %copy-done.3, bf16[256,2048]{1,0:T(8,128)(2,1)} %copy-done, bf16[2048,3584]{1,0:T(8,128)(2,1)} %refs_1_.7, bf16[2048,3584]{1,0:T(8,128)(2,1)} %refs_2_.7, bf16[3584,2048]{1,0:T(8,128)(2,1)} %down.7, ...), custom_call_target="tpu_custom_call" | custom-call | flops 1 | bytes 1 | tf_op jit(solution)/shard_map/pallas_call | solution.py:112
  54.7 3.6 %shard_map.106 = bf16[3,64,1024]{2,1,0:T(8,128)(2,1)} custom-call(f32[3,64,1024]{2,1,0:T(8,128)} %slice.111.mine, bf16[3,64,1024]{2,1,0:T(8,128)(2,1)} %collective-permute-done.6.received, f32[64,1]{1,0:T(8,128)} %copy-done.8), custom_call_target="tpu_custom_call" | custom-call | flops 1 | bytes 1 | tf_op jit(solution)/shard_map/pallas_call | solution.py:143
  58.3 1.7 collective-permute-start.7
  59.9 1.8 convert_add_fusion
  61.8 1.6 collective-permute-start.15
  63.4 7.4 %shard_map.105 = (f32[3,128,768]{2,1,0:T(8,128)}, bf16[3,128,768]{2,1,0:T(8,128)(2,1)S(1)}) custom-call(bf16[256,2048]{1,0:T(8,128)(2,1)S(1)} %copy-done.4, bf16[256,2048]{1,0:T(8,128)(2,1)} %copy-done, bf16[2048,3584]{1,0:T(8,128)(2,1)} %refs_1_.7, bf16[2048,3584]{1,0:T(8,128)(2,1)} %refs_2_.7, bf16[3584,2048]{1,0:T(8,128)(2,1)} %down.7, ...), custom_call_target="tpu_custom_call" | custom-call | flops 1 | bytes 1 | tf_op jit(solution)/shard_map/pallas_call | solution.py:112
  71.3 1.0 pad_maximum_fusion.7
  73.6 4.4 %collective-permute-done.15.received = bf16[3,64,1024]{2,1,0:T(8,128)(2,1)S(1)} collective-permute-done((bf16[3,64,1024]{2,1,0:T(8,128)(2,1)S(1)}, bf16[3,64,1024]{2,1,0:T(8,128)(2,1)S(1)}, u32[]{:S(2)}, u32[]{:S(2)}) %collective-permute-start.15) | collective-permute-done | bytes 393248 | tf_op jit(solution)/shard_map/ppermute | solution.py:16
  78.8 3.6 %shard_map.110 = bf16[3,64,1024]{2,1,0:T(8,128)(2,1)} custom-call(f32[3,64,1024]{2,1,0:T(8,128)} %slice.119.mine, bf16[3,64,1024]{2,1,0:T(8,128)(2,1)} %copy-done.24, f32[64,1]{1,0:T(8,128)} %copy-done.8), custom_call_target="tpu_custom_call" | custom-call | flops 1 | bytes 1 | tf_op jit(solution)/shard_map/pallas_call | solution.py:143
  82.9 1.3 convert_add_fusion.2
  85.4 1.2 convert_add_fusion.3
  87.3 1.7 collective-permute-start.5
  89.1 14.3 %collective-permute-done.16 = bf16[3,64,1024]{2,1,0:T(8,128)(2,1)S(1)} collective-permute-done((bf16[3,64,1024]{2,1,0:T(8,128)(2,1)}, bf16[3,64,1024]{2,1,0:T(8,128)(2,1)S(1)}, u32[]{:S(2)}, u32[]{:S(2)}) %collective-permute-start.16) | collective-permute-done | bytes 393248 | tf_op jit(solution)/shard_map/ppermute | solution.py:16
  103.3 1.0 pad_maximum_fusion.8
  105.6 3.0 %shard_map.109 = bf16[3,64,768]{2,1,0:T(8,128)(2,1)} custom-call(f32[3,64,768]{2,1,0:T(8,128)} %slice.115.mine, bf16[3,64,768]{2,1,0:T(8,128)(2,1)} %copy-done.25, f32[64,1]{1,0:T(8,128)} %copy-done.8), custom_call_target="tpu_custom_call" | custom-call | flops 1 | bytes 1 | tf_op jit(solution)/shard_map/pallas_call | solution.py:143
  108.5 1.5 collective-permute-start.13
  110.1 1.2 fusion.2
  111.3 2.6 %pad_maximum_fusion.1.refs_0_ = bf16[3,256,1024]{2,1,0:T(8,128)(2,1)} fusion(bf16[3,64,1024]{2,1,0:T(8,128)(2,1)S(1)} %get-tuple-element.82, bf16[3,64,1024]{2,1,0:T(8,128)(2,1)} %copy-done.19, bf16[3,64,1024]{2,1,0:T(8,128)(2,1)S(1)} %get-tuple-element.81, bf16[3,64,1024]{2,1,0:T(8,128)(2,1)} %shard_map.106), kind=kLoop, calls=%fused_computation.3 | loop fusion | flops 6291456 | bytes 3145728 | tf_op jit(solution)/shard_map/concatenate | solution.py:68
  114.7 11.8 %shard_map.107 = (f32[256,2048]{1,0:T(8,128)}, bf16[2048,3584]{1,0:T(8,128)(2,1)}, bf16[2048,3584]{1,0:T(8,128)(2,1)}, bf16[3584,2048]{1,0:T(8,128)(2,1)}) custom-call(bf16[3,256,1024]{2,1,0:T(8,128)(2,1)} %pad_maximum_fusion.1.refs_0_, bf16[2048,3584]{1,0:T(8,128)(2,1)} %refs_1_.7, bf16[2048,3584]{1,0:T(8,128)(2,1)} %refs_2_.7, ...), custom_call_target="tpu_custom_call" | custom-call | flops 1 | bytes 1 | tf_op jit(solution)/shard_map/pallas_call | solution.py:273
  126.5 3.0 %shard_map.108 = bf16[3,64,768]{2,1,0:T(8,128)(2,1)} custom-call(f32[3,64,768]{2,1,0:T(8,128)} %slice.109.mine, bf16[3,64,768]{2,1,0:T(8,128)(2,1)} %collective-permute-done.5.received, f32[64,1]{1,0:T(8,128)} %copy-done.8, bf16[2048,3584]{1,0:T(8,128)(2,1)} %get-tuple-element.37.rest_0_.refs_6_), custom_call_target="tpu_custom_call" | custom-call | flops 1 | bytes 1 | tf_op jit(solution)/shard_map/pallas_call | solution.py:143
  130.1 1.9 pad_maximum_fusion.10
  131.9 1.5 collective-permute-start.14
  133.5 5.8 %collective-permute-done.9 = bf16[3,64,768]{2,1,0:T(8,128)(2,1)S(1)} collective-permute-done((bf16[3,64,768]{2,1,0:T(8,128)(2,1)}, bf16[3,64,768]{2,1,0:T(8,128)(2,1)S(1)}, u32[]{:S(2)}, u32[]{:S(2)}) %collective-permute-start.9) | collective-permute-done | bytes 294944 | tf_op jit(solution)/shard_map/ppermute | solution.py:16
  139.3 1.8 pad_maximum_fusion.9
  141.5 2.5 %pad_maximum_fusion.2.refs_0_ = bf16[3,256,1024]{2,1,0:T(8,128)(2,1)} fusion(bf16[3,128,1024]{2,1,0:T(8,128)(2,1)} %collective-permute-done.17, bf16[3,64,1024]{2,1,0:T(8,128)(2,1)S(1)} %copy-done.18, bf16[3,64,1024]{2,1,0:T(8,128)(2,1)S(1)} %copy-done.12), kind=kLoop, calls=%fused_computation.4 | loop fusion | flops 4718592 | bytes 3145728 | tf_op jit(solution)/shard_map/concatenate | solution.py:68
  144.0 12.8 %shard_map.111 = (f32[256,2048]{1,0:T(8,128)}, bf16[2048,3584]{1,0:T(8,128)(2,1)}, bf16[2048,3584]{1,0:T(8,128)(2,1)}, bf16[3584,2048]{1,0:T(8,128)(2,1)}) custom-call(bf16[3,256,1024]{2,1,0:T(8,128)(2,1)} %pad_maximum_fusion.2.refs_0_, bf16[2048,3584]{1,0:T(8,128)(2,1)} %refs_1_.7, ...), custom_call_target="tpu_custom_call", output_to_operand_aliasing={{1}: (6, {}), {2}: (7, {}), {3}: (8, {})} | custom-call | flops 1 | bytes 1 | tf_op jit(solution)/shard_map/pallas_call | solution.py:273
  156.9 1.1 fusion.3
  158.0 2.1 pad_maximum_fusion.4.refs_0_
  160.1 11.5 %shard_map.112 = (f32[256,2048]{1,0:T(8,128)}, bf16[2048,3584]{1,0:T(8,128)(2,1)}, bf16[2048,3584]{1,0:T(8,128)(2,1)}, bf16[3584,2048]{1,0:T(8,128)(2,1)}) custom-call(bf16[3,256,768]{2,1,0:T(8,128)(2,1)} %pad_maximum_fusion.4.refs_0_, bf16[2048,3584]{1,0:T(8,128)(2,1)} %refs_1_.7, ...), custom_call_target="tpu_custom_call", output_to_operand_aliasing={{1}: (6, {}), {2}: (7, {}), {3}: (8, {})} | custom-call | flops 1 | bytes 1 | tf_op jit(solution)/shard_map/pallas_call | solution.py:273
  171.6 1.1 pad_maximum_fusion.3.refs_0_
  172.8 7.3 %shard_map.113 = f32[256,2048]{1,0:T(8,128)} custom-call(bf16[3,256,768]{2,1,0:T(8,128)(2,1)S(1)} %pad_maximum_fusion.3.refs_0_, bf16[2048,3584]{1,0:T(8,128)(2,1)} %refs_1_.7, bf16[2048,3584]{1,0:T(8,128)(2,1)} %refs_2_.7, f32[256,2048]{1,0:T(8,128)} %get-tuple-element.47.refs_3_), custom_call_target="tpu_custom_call" | custom-call | flops 1 | bytes 1 | tf_op jit(solution)/shard_map/pallas_call | solution.py:273
  180.0 1.7 constant_dynamic-slice_fusion.12
  182.3 1.6 constant_dynamic-slice_fusion.hidden
  183.9 1.1 collective-permute-done.18
  185.2 1.7 collective-permute-start.19
  187.0 6.7 %collective-permute-done.19 = bf16[64,2048]{1,0:T(8,128)(2,1)S(1)} collective-permute-done((bf16[64,2048]{1,0:T(8,128)(2,1)S(1)}, bf16[64,2048]{1,0:T(8,128)(2,1)S(1)}, u32[]{:S(2)}, u32[]{:S(2)}) %collective-permute-start.19) | collective-permute-done | bytes 262176 | tf_op jit(solution)/shard_map/ppermute | solution.py:16
  193.7 2.7 %collective-permute-start.20 = (bf16[32,2048]{1,0:T(8,128)(2,1)S(1)}, bf16[32,2048]{1,0:T(8,128)(2,1)S(1)}, u32[]{:S(2)}, u32[]{:S(2)}) collective-permute-start(bf16[32,2048]{1,0:T(8,128)(2,1)S(1)} %slice.148), channel_id=1, source_target_pairs={{0,16},{4,20},{8,24},{12,28},{16,0},{20,4},{24,8},{28,12},{1,17},{... | collective-permute-start | bytes 393224 | tf_op jit(solution)/shard_map/ppermute | solution.py:16
  196.4 5.7 %shard_map.114 = (bf16[2048,3584]{1,0:T(8,128)(2,1)}, bf16[2048,3584]{1,0:T(8,128)(2,1)}, bf16[3584,2048]{1,0:T(8,128)(2,1)}) custom-call(bf16[3,256,768]{2,1,0:T(8,128)(2,1)} %copy-done.5, bf16[2048,256]{1,0:T(8,128)(2,1)S(1)} %copy-done.2, bf16[256,2048]{1,0:T(8,128)(2,1)S(1)} %copy-done.1, ...), custom_call_target="tpu_custom_call", output_to_operand_aliasing={{0}: (3, {}), {1}: (4, {}), {2}: (5, {})} | custom-call | flops 2415919104 | bytes 9437184 | tf_op jit(solution)/shard_map/pallas_call | solution.py:273
  203.5 1.8 shard_map.115
  206.6 3.1 %collective-permute-done.21 = f32[32]{0:T(128)S(1)} collective-permute-done((f32[32]{0:T(128)S(1)}, f32[32]{0:T(128)S(1)}, u32[]{:S(2)}, u32[]{:S(2)}) %collective-permute-start.21) | collective-permute-done | bytes 160 | tf_op jit(solution)/shard_map/ppermute | solution.py:16
  209.7 1.5 collective-permute-start.22
  212.0 1.6 collective-permute-start.24
  214.3 1.3 collective-permute-done.24
  216.2 1.8 shard_map.116
  218.0 1.5 collective-permute-start.25
  219.5 6.0 %collective-permute-done.25 = bf16[32,2048]{1,0:T(8,128)(2,1)S(1)} collective-permute-done((bf16[32,2048]{1,0:T(8,128)(2,1)}, bf16[32,2048]{1,0:T(8,128)(2,1)S(1)}, u32[]{:S(2)}, u32[]{:S(2)}) %collective-permute-start.25) | collective-permute-done | bytes 131104 | tf_op jit(solution)/shard_map/ppermute | solution.py:16
  226.8 6.1 %collective-permute-done.26 = bf16[64,2048]{1,0:T(8,128)(2,1)S(1)} collective-permute-done((bf16[64,2048]{1,0:T(8,128)(2,1)S(1)}, bf16[64,2048]{1,0:T(8,128)(2,1)S(1)}, u32[]{:S(2)}, u32[]{:S(2)}) %collective-permute-start.26) | collective-permute-done | bytes 262176 | tf_op jit(solution)/shard_map/ppermute | solution.py:16
  233.9 1.0 collective-permute-start.28
  234.9 3.6 %collective-permute-done.28 = f32[2048]{0:T(1024)S(1)} collective-permute-done((f32[2048]{0:T(1024)S(1)}, f32[2048]{0:T(1024)S(1)}, u32[]{:S(2)}, u32[]{:S(2)}) %collective-permute-start.28) | collective-permute-done | bytes 8224 | tf_op jit(solution)/shard_map/ppermute | solution.py:16
  239.5 1.0 copy-done.29
  (139 shorter events, 20.2 us)
Async XLA Ops:
  0.6 5.9 %copy-start.23 = (bf16[256,2048]{1,0:T(8,128)(2,1)S(1)}, bf16[256,2048]{1,0:T(8,128)(2,1)}, u32[]{:S(2)}) copy-start(bf16[256,2048]{1,0:T(8,128)(2,1)} %param.8) | copy-start | bytes 3145732
  2.2 4.8 %collective-permute-start = (f32[256]{0:T(256)S(1)}, f32[256]{0:T(256)S(1)}, u32[]{:S(2)}, u32[]{:S(2)}) collective-permute-start(f32[256]{0:T(256)S(1)} %multiply_reduce_fusion), channel_id=1, source_target_pairs={{0,1},{1,0},{2,3},{3,2},{4,5},{5,4},{6,7},{7,6},{8,9},{9,8},{10,11... | collective-permute-start | bytes 3080 | tf_op jit(solution)/shard_map/ppermute | solution.py:16
  5.2 1.4 copy-start.27
  6.9 13.8 %copy-start.3 = (bf16[256,2048]{1,0:T(8,128)(2,1)}, bf16[256,2048]{1,0:T(8,128)(2,1)S(1)}, u32[]{:S(2)}) copy-start(bf16[256,2048]{1,0:T(8,128)(2,1)S(1)} %multiply_convert_fusion.scaled.x) | copy-start | bytes 3145732
  7.0 8.7 %copy-start = (bf16[256,2048]{1,0:T(8,128)(2,1)}, bf16[256,2048]{1,0:T(8,128)(2,1)S(1)}, u32[]{:S(2)}) copy-start(bf16[256,2048]{1,0:T(8,128)(2,1)S(1)} %pad_maximum_fusion.5.grad_out.refs_4_.refs_5_.refs_2_) | copy-start | bytes 3145732
  15.7 19.2 %collective-permute-start.2 = (bf16[3,128,1024]{2,1,0:T(8,128)(2,1)}, bf16[3,128,1024]{2,1,0:T(8,128)(2,1)S(1)}, u32[]{:S(2)}, u32[]{:S(2)}) collective-permute-start(bf16[3,128,1024]{2,1,0:T(8,128)(2,1)} %get-tuple-element.31.rest_0_), channel_id=1, source_target_pairs={{0,1},{1,0},{2,3},{3,2},{4,5},{5,4},{6,7},{7,6},{8,9},{9,8},{10,11... | collective-permute-start | bytes 2359304 | tf_op jit(solution)/shard_map/ppermute | solution.py:16
  16.9 3.6 %collective-permute-start.1 = (f32[256]{0:T(256)S(1)}, f32[256]{0:T(256)S(1)}, u32[]{:S(2)}, u32[]{:S(2)}) collective-permute-start(f32[256]{0:T(256)S(1)} %add.104), channel_id=1, source_target_pairs={{0,2},{1,3},{2,0},{3,1},{4,6},{5,7},{6,4},{7,5},{8,10},{9,11},{10,... | collective-permute-start | bytes 3080 | tf_op jit(solution)/shard_map/ppermute | solution.py:16
  20.7 8.7 %copy-start.8 = (f32[64,1]{1,0:T(8,128)}, f32[64,1]{1,0:T(8,128)S(1)}, u32[]{:S(2)}) copy-start(f32[64,1]{1,0:T(8,128)S(1)} %copy.26.rest_1_.inverse) | copy-start | bytes 772
  20.7 14.3 %copy-start.20 = (f32[3,128,1024]{2,1,0:T(8,128)S(1)}, f32[3,128,1024]{2,1,0:T(8,128)}, u32[]{:S(2)}) copy-start(f32[3,128,1024]{2,1,0:T(8,128)} %get-tuple-element.36) | copy-start | bytes 4718596
  29.4 8.6 %copy-start.6 = (bf16[3,128,1024]{2,1,0:T(8,128)(2,1)}, bf16[3,128,1024]{2,1,0:T(8,128)(2,1)S(1)}, u32[]{:S(2)}) copy-start(bf16[3,128,1024]{2,1,0:T(8,128)(2,1)S(1)} %get-tuple-element.32.after.rest_0_) | copy-start | bytes 2359300
  29.4 30.6 %collective-permute-start.3 = (bf16[3,128,1024]{2,1,0:T(8,128)(2,1)S(1)}, bf16[3,128,1024]{2,1,0:T(8,128)(2,1)S(1)}, u32[]{:S(2)}, u32[]{:S(2)}) collective-permute-start(bf16[3,128,1024]{2,1,0:T(8,128)(2,1)S(1)} %get-tuple-element.32.after.rest_0_), channel_id=1, source_target_pairs={{0,2},{1,3},{2,0},{3,1},{4,6},{5,7},{6,4},{7,5},{8,10},{9,11},{10,... | collective-permute-start | bytes 2359304 | tf_op jit(solution)/shard_map/ppermute | solution.py:16
  35.2 1.1 copy-start.9
  36.4 18.3 %collective-permute-start.6 = (bf16[3,64,1024]{2,1,0:T(8,128)(2,1)S(1)}, bf16[3,64,1024]{2,1,0:T(8,128)(2,1)}, u32[]{:S(2)}, u32[]{:S(2)}) collective-permute-start(bf16[3,64,1024]{2,1,0:T(8,128)(2,1)S(1)} %slice.145), channel_id=1, source_target_pairs={{0,2},{1,3},{2,0},{3,1},{4,6},{5,7},{6,4},{7,5},{8,10},{9,11},{10,... | collective-permute-start | bytes 1179656 | tf_op jit(solution)/shard_map/ppermute | solution.py:16
  43.4 1.1 copy-start.7
  44.5 7.8 %copy-start.10 = (f32[3,128,1024]{2,1,0:T(8,128)S(1)}, f32[3,128,1024]{2,1,0:T(8,128)}, u32[]{:S(2)}) copy-start(f32[3,128,1024]{2,1,0:T(8,128)} %copy-done.9) | copy-start | bytes 4718596
  53.3 29.5 %collective-permute-start.11 = (bf16[3,128,768]{2,1,0:T(8,128)(2,1)S(1)}, bf16[3,128,768]{2,1,0:T(8,128)(2,1)}, u32[]{:S(2)}, u32[]{:S(2)}) collective-permute-start(bf16[3,128,768]{2,1,0:T(8,128)(2,1)S(1)} %get-tuple-element.33.rest_0_), channel_id=1, source_target_pairs={{0,1},{1,0},{2,3},{3,2},{4,5},{5,4},{6,7},{7,6},{8,9},{9,8},{10,11... | collective-permute-start | bytes 1769480 | tf_op jit(solution)/shard_map/ppermute | solution.py:16
  58.3 13.0 %collective-permute-start.7 = (bf16[3,64,1024]{2,1,0:T(8,128)(2,1)}, bf16[3,64,1024]{2,1,0:T(8,128)(2,1)S(1)}, u32[]{:S(2)}, u32[]{:S(2)}) collective-permute-start(bf16[3,64,1024]{2,1,0:T(8,128)(2,1)} %shard_map.106), channel_id=1, source_target_pairs={{0,2},{1,3},{2,0},{3,1},{4,6},{5,7},{6,4},{7,5},{8,10},{9,11},{10,... | collective-permute-start | bytes 1179656 | tf_op jit(solution)/shard_map/ppermute | solution.py:16
  59.9 3.5 %copy-start.4 = (bf16[256,2048]{1,0:T(8,128)(2,1)S(1)}, bf16[256,2048]{1,0:T(8,128)(2,1)}, u32[]{:S(2)}) copy-start(bf16[256,2048]{1,0:T(8,128)(2,1)} %copy-done.3) | copy-start | bytes 3145732
  61.8 9.5 %copy-start.13 = (bf16[3,64,1024]{2,1,0:T(8,128)(2,1)S(1)}, bf16[3,64,1024]{2,1,0:T(8,128)(2,1)}, u32[]{:S(2)}) copy-start(bf16[3,64,1024]{2,1,0:T(8,128)(2,1)} %shard_map.106) | copy-start | bytes 1179652
  61.8 16.2 %collective-permute-start.15 = (bf16[3,64,1024]{2,1,0:T(8,128)(2,1)S(1)}, bf16[3,64,1024]{2,1,0:T(8,128)(2,1)S(1)}, u32[]{:S(2)}, u32[]{:S(2)}) collective-permute-start(bf16[3,64,1024]{2,1,0:T(8,128)(2,1)S(1)} %slice.144), channel_id=1, source_target_pairs={{0,1},{1,0},{2,3},{3,2},{4,5},{5,4},{6,7},{7,6},{8,9},{9,8},{10,11... | collective-permute-start | bytes 1179656 | tf_op jit(solution)/shard_map/ppermute | solution.py:16
  70.8 12.1 %copy-start.21 = (f32[3,128,768]{2,1,0:T(8,128)S(1)}, f32[3,128,768]{2,1,0:T(8,128)}, u32[]{:S(2)}) copy-start(f32[3,128,768]{2,1,0:T(8,128)} %get-tuple-element.38) | copy-start | bytes 3538948
  70.8 14.6 %collective-permute-start.4 = (bf16[3,128,768]{2,1,0:T(8,128)(2,1)S(1)}, bf16[3,128,768]{2,1,0:T(8,128)(2,1)}, u32[]{:S(2)}, u32[]{:S(2)}) collective-permute-start(bf16[3,128,768]{2,1,0:T(8,128)(2,1)S(1)} %get-tuple-element.35), channel_id=1, source_target_pairs={{0,2},{1,3},{2,0},{3,1},{4,6},{5,7},{6,4},{7,5},{8,10},{9,11},{10,... | collective-permute-start | bytes 1769480 | tf_op jit(solution)/shard_map/ppermute | solution.py:16
  71.3 2.3 copy-start.19
  72.3 37.8 %collective-permute-start.8 = (bf16[3,128,1024]{2,1,0:T(8,128)(2,1)}, bf16[3,128,1024]{2,1,0:T(8,128)(2,1)}, u32[]{:S(2)}, u32[]{:S(2)}) collective-permute-start(bf16[3,128,1024]{2,1,0:T(8,128)(2,1)} %pad_maximum_fusion.7), channel_id=1, source_target_pairs={{0,1},{1,0},{2,3},{3,2},{4,5},{5,4},{6,7},{7,6},{8,9},{9,8},{10,11... | collective-permute-start | bytes 2359304 | tf_op jit(solution)/shard_map/ppermute | solution.py:16
  78.0 0.8 copy-start.24
  82.4 20.9 %collective-permute-start.16 = (bf16[3,64,1024]{2,1,0:T(8,128)(2,1)}, bf16[3,64,1024]{2,1,0:T(8,128)(2,1)S(1)}, u32[]{:S(2)}, u32[]{:S(2)}) collective-permute-start(bf16[3,64,1024]{2,1,0:T(8,128)(2,1)} %shard_map.110), channel_id=1, source_target_pairs={{0,1},{1,0},{2,3},{3,2},{4,5},{5,4},{6,7},{7,6},{8,9},{9,8},{10,11... | collective-permute-start | bytes 1179656 | tf_op jit(solution)/shard_map/ppermute | solution.py:16
  82.9 2.5 %copy-start.22 = (f32[3,128,768]{2,1,0:T(8,128)S(1)}, f32[3,128,768]{2,1,0:T(8,128)}, u32[]{:S(2)}) copy-start(f32[3,128,768]{2,1,0:T(8,128)} %get-tuple-element.34) | copy-start | bytes 3538948
  84.2 19.1 %copy-start.11 = (bf16[3,64,1024]{2,1,0:T(8,128)(2,1)S(1)}, bf16[3,64,1024]{2,1,0:T(8,128)(2,1)}, u32[]{:S(2)}) copy-start(bf16[3,64,1024]{2,1,0:T(8,128)(2,1)} %shard_map.110) | copy-start | bytes 1179652
  85.1 19.8 %collective-permute-start.12 = (bf16[3,64,768]{2,1,0:T(8,128)(2,1)S(1)}, bf16[3,64,768]{2,1,0:T(8,128)(2,1)S(1)}, u32[]{:S(2)}, u32[]{:S(2)}) collective-permute-start(bf16[3,64,768]{2,1,0:T(8,128)(2,1)S(1)} %slice.146), channel_id=1, source_target_pairs={{0,2},{1,3},{2,0},{3,1},{4,6},{5,7},{6,4},{7,5},{8,10},{9,11},{10,... | collective-permute-start | bytes 884744 | tf_op jit(solution)/shard_map/ppermute | solution.py:16
  87.3 39.2 %collective-permute-start.5 = (bf16[3,64,768]{2,1,0:T(8,128)(2,1)}, bf16[3,64,768]{2,1,0:T(8,128)(2,1)}, u32[]{:S(2)}, u32[]{:S(2)}) collective-permute-start(bf16[3,64,768]{2,1,0:T(8,128)(2,1)} %slice.147), channel_id=1, source_target_pairs={{0,1},{1,0},{2,3},{3,2},{4,5},{5,4},{6,7},{7,6},{8,9},{9,8},{10,11... | collective-permute-start | bytes 884744 | tf_op jit(solution)/shard_map/ppermute | solution.py:16
  103.3 7.9 %copy-start.17 = (bf16[3,64,1024]{2,1,0:T(8,128)(2,1)}, bf16[3,64,1024]{2,1,0:T(8,128)(2,1)S(1)}, u32[]{:S(2)}) copy-start(bf16[3,64,1024]{2,1,0:T(8,128)(2,1)S(1)} %collective-permute-done.16) | copy-start | bytes 1179652
  104.3 37.2 %collective-permute-start.17 = (bf16[3,128,1024]{2,1,0:T(8,128)(2,1)}, bf16[3,128,1024]{2,1,0:T(8,128)(2,1)}, u32[]{:S(2)}, u32[]{:S(2)}) collective-permute-start(bf16[3,128,1024]{2,1,0:T(8,128)(2,1)} %pad_maximum_fusion.8), channel_id=1, source_target_pairs={{0,2},{1,3},{2,0},{3,1},{4,6},{5,7},{6,4},{7,5},{8,10},{9,11},{10,... | collective-permute-start | bytes 2359304 | tf_op jit(solution)/shard_map/ppermute | solution.py:16
  104.9 0.7 copy-start.25
  108.5 21.5 %collective-permute-start.13 = (bf16[3,64,768]{2,1,0:T(8,128)(2,1)}, bf16[3,64,768]{2,1,0:T(8,128)(2,1)}, u32[]{:S(2)}, u32[]{:S(2)}) collective-permute-start(bf16[3,64,768]{2,1,0:T(8,128)(2,1)} %shard_map.109), channel_id=1, source_target_pairs={{0,2},{1,3},{2,0},{3,1},{4,6},{5,7},{6,4},{7,5},{8,10},{9,11},{10,... | collective-permute-start | bytes 884744 | tf_op jit(solution)/shard_map/ppermute | solution.py:16
  111.2 3.5 %copy-start.1 = (bf16[256,2048]{1,0:T(8,128)(2,1)S(1)}, bf16[256,2048]{1,0:T(8,128)(2,1)}, u32[]{:S(2)}) copy-start(bf16[256,2048]{1,0:T(8,128)(2,1)} %copy-done) | copy-start | bytes 3145732
  111.2 3.5 %copy-start.2 = (bf16[2048,256]{1,0:T(8,128)(2,1)S(1)}, bf16[2048,256]{1,0:T(8,128)(2,1)}, u32[]{:S(2)}) copy-start(bf16[2048,256]{1,0:T(8,128)(2,1)} %shard_map.103.rest_2_.refs_3_.refs_4_.refs_1_) | copy-start | bytes 3145732
  126.5 3.5 %copy-start.14 = (bf16[3,64,768]{2,1,0:T(8,128)(2,1)S(1)}, bf16[3,64,768]{2,1,0:T(8,128)(2,1)}, u32[]{:S(2)}) copy-start(bf16[3,64,768]{2,1,0:T(8,128)(2,1)} %shard_map.109) | copy-start | bytes 884740
  129.6 12.0 %copy-start.12 = (bf16[3,64,1024]{2,1,0:T(8,128)(2,1)S(1)}, bf16[3,64,1024]{2,1,0:T(8,128)(2,1)}, u32[]{:S(2)}) copy-start(bf16[3,64,1024]{2,1,0:T(8,128)(2,1)} %shard_map.110) | copy-start | bytes 1179652
  129.6 12.0 %copy-start.18 = (bf16[3,64,1024]{2,1,0:T(8,128)(2,1)S(1)}, bf16[3,64,1024]{2,1,0:T(8,128)(2,1)}, u32[]{:S(2)}) copy-start(bf16[3,64,1024]{2,1,0:T(8,128)(2,1)} %copy-done.17) | copy-start | bytes 1179652
  129.6 9.7 %collective-permute-start.9 = (bf16[3,64,768]{2,1,0:T(8,128)(2,1)}, bf16[3,64,768]{2,1,0:T(8,128)(2,1)S(1)}, u32[]{:S(2)}, u32[]{:S(2)}) collective-permute-start(bf16[3,64,768]{2,1,0:T(8,128)(2,1)} %shard_map.108), channel_id=1, source_target_pairs={{0,1},{1,0},{2,3},{3,2},{4,5},{5,4},{6,7},{7,6},{8,9},{9,8},{10,11... | collective-permute-start | bytes 884744 | tf_op jit(solution)/shard_map/ppermute | solution.py:16
  131.9 24.9 %collective-permute-start.14 = (bf16[3,128,768]{2,1,0:T(8,128)(2,1)}, bf16[3,128,768]{2,1,0:T(8,128)(2,1)}, u32[]{:S(2)}, u32[]{:S(2)}) collective-permute-start(bf16[3,128,768]{2,1,0:T(8,128)(2,1)} %pad_maximum_fusion.10), channel_id=1, source_target_pairs={{0,1},{1,0},{2,3},{3,2},{4,5},{5,4},{6,7},{7,6},{8,9},{9,8},{10,11... | collective-permute-start | bytes 1769480 | tf_op jit(solution)/shard_map/ppermute | solution.py:16
  141.1 30.5 %collective-permute-start.10 = (bf16[3,128,768]{2,1,0:T(8,128)(2,1)}, bf16[3,128,768]{2,1,0:T(8,128)(2,1)}, u32[]{:S(2)}, u32[]{:S(2)}) collective-permute-start(bf16[3,128,768]{2,1,0:T(8,128)(2,1)} %pad_maximum_fusion.9), channel_id=1, source_target_pairs={{0,2},{1,3},{2,0},{3,1},{4,6},{5,7},{6,4},{7,5},{8,10},{9,11},{10,... | collective-permute-start | bytes 1769480 | tf_op jit(solution)/shard_map/ppermute | solution.py:16
  160.1 11.5 %copy-start.15 = (bf16[3,64,768]{2,1,0:T(8,128)(2,1)S(1)}, bf16[3,64,768]{2,1,0:T(8,128)(2,1)}, u32[]{:S(2)}) copy-start(bf16[3,64,768]{2,1,0:T(8,128)(2,1)} %shard_map.108) | copy-start | bytes 884740
  172.8 7.3 %copy-start.5 = (bf16[3,256,768]{2,1,0:T(8,128)(2,1)}, bf16[3,256,768]{2,1,0:T(8,128)(2,1)S(1)}, u32[]{:S(2)}) copy-start(bf16[3,256,768]{2,1,0:T(8,128)(2,1)S(1)} %pad_maximum_fusion.3.refs_0_) | copy-start | bytes 3538948
  182.3 2.7 %collective-permute-start.18 = (f32[128,2048]{1,0:T(8,128)S(1)}, f32[128,2048]{1,0:T(8,128)S(1)}, u32[]{:S(2)}, u32[]{:S(2)}) collective-permute-start(f32[128,2048]{1,0:T(8,128)S(1)} %pad_maximum_fusion.6), channel_id=1, source_target_pairs={{0,4},{4,0},{8,12},{12,8},{16,20},{20,16},{24,28},{28,24},{1,5},{5... | collective-permute-start | bytes 3145736 | tf_op jit(solution)/shard_map/ppermute | solution.py:16
  185.2 8.4 %collective-permute-start.19 = (bf16[64,2048]{1,0:T(8,128)(2,1)S(1)}, bf16[64,2048]{1,0:T(8,128)(2,1)S(1)}, u32[]{:S(2)}, u32[]{:S(2)}) collective-permute-start(bf16[64,2048]{1,0:T(8,128)(2,1)S(1)} %pad_maximum_fusion.12), channel_id=1, source_target_pairs={{0,8},{4,12},{8,0},{12,4},{16,24},{20,28},{24,16},{28,20},{1,9},{5... | collective-permute-start | bytes 786440 | tf_op jit(solution)/shard_map/ppermute | solution.py:16
  193.7 9.1 %collective-permute-start.20 = (bf16[32,2048]{1,0:T(8,128)(2,1)S(1)}, bf16[32,2048]{1,0:T(8,128)(2,1)S(1)}, u32[]{:S(2)}, u32[]{:S(2)}) collective-permute-start(bf16[32,2048]{1,0:T(8,128)(2,1)S(1)} %slice.148), channel_id=1, source_target_pairs={{0,16},{4,20},{8,24},{12,28},{16,0},{20,4},{24,8},{28,12},{1,17},{... | collective-permute-start | bytes 393224 | tf_op jit(solution)/shard_map/ppermute | solution.py:16
  202.8 0.6 copy-start.26
  205.3 6.0 %collective-permute-start.23 = (f32[2048]{0:T(1024)}, f32[2048]{0:T(1024)S(1)}, u32[]{:S(2)}, u32[]{:S(2)}) collective-permute-start(f32[2048]{0:T(1024)} %bitcast.12), channel_id=1, source_target_pairs={{0,4},{4,0},{8,12},{12,8},{16,20},{20,16},{24,28},{28,24},{1,5},{5... | collective-permute-start | bytes 24584 | tf_op jit(solution)/shard_map/ppermute | solution.py:16
  206.1 3.6 %collective-permute-start.21 = (f32[32]{0:T(128)S(1)}, f32[32]{0:T(128)S(1)}, u32[]{:S(2)}, u32[]{:S(2)}) collective-permute-start(f32[32]{0:T(128)S(1)} %reduce), channel_id=1, source_target_pairs={{0,1},{1,0},{2,3},{3,2},{4,5},{5,4},{6,7},{7,6},{8,9},{9,8},{10,11... | collective-permute-start | bytes 392 | tf_op jit(solution)/shard_map/ppermute | solution.py:16
  209.7 3.8 %collective-permute-start.22 = (f32[32]{0:T(128)S(1)}, f32[32]{0:T(128)S(1)}, u32[]{:S(2)}, u32[]{:S(2)}) collective-permute-start(f32[32]{0:T(128)S(1)} %add.122), channel_id=1, source_target_pairs={{0,2},{1,3},{2,0},{3,1},{4,6},{5,7},{6,4},{7,5},{8,10},{9,11},{10,... | collective-permute-start | bytes 392 | tf_op jit(solution)/shard_map/ppermute | solution.py:16
  212.0 3.7 %collective-permute-start.24 = (f32[2048]{0:T(1024)S(1)}, f32[2048]{0:T(1024)S(1)}, u32[]{:S(2)}, u32[]{:S(2)}) collective-permute-start(f32[2048]{0:T(1024)S(1)} %add.124), channel_id=1, source_target_pairs={{0,8},{4,12},{8,0},{12,4},{16,24},{20,28},{24,16},{28,20},{1,9},{5... | collective-permute-start | bytes 24584 | tf_op jit(solution)/shard_map/ppermute | solution.py:16
  216.2 17.7 %copy-start.28 = (f32[2048]{0:T(1024)S(1)}, f32[2048]{0:T(1024)}, u32[]{:S(2)}) copy-start(f32[2048]{0:T(1024)} %add.125) | copy-start | bytes 24580
  218.0 16.9 %copy-start.16 = (bf16[32,2048]{1,0:T(8,128)(2,1)S(1)}, bf16[32,2048]{1,0:T(8,128)(2,1)}, u32[]{:S(2)}) copy-start(bf16[32,2048]{1,0:T(8,128)(2,1)} %shard_map.116) | copy-start | bytes 393220
  218.0 7.5 %collective-permute-start.25 = (bf16[32,2048]{1,0:T(8,128)(2,1)}, bf16[32,2048]{1,0:T(8,128)(2,1)S(1)}, u32[]{:S(2)}, u32[]{:S(2)}) collective-permute-start(bf16[32,2048]{1,0:T(8,128)(2,1)} %shard_map.116), channel_id=1, source_target_pairs={{0,16},{4,20},{8,24},{12,28},{16,0},{20,4},{24,8},{28,12},{1,17},{... | collective-permute-start | bytes 393224 | tf_op jit(solution)/shard_map/ppermute | solution.py:16
  226.4 6.4 %collective-permute-start.26 = (bf16[64,2048]{1,0:T(8,128)(2,1)S(1)}, bf16[64,2048]{1,0:T(8,128)(2,1)S(1)}, u32[]{:S(2)}, u32[]{:S(2)}) collective-permute-start(bf16[64,2048]{1,0:T(8,128)(2,1)S(1)} %pad_maximum_fusion.13), channel_id=1, source_target_pairs={{0,8},{4,12},{8,0},{12,4},{16,24},{20,28},{24,16},{28,20},{1,9},{5... | collective-permute-start | bytes 786440 | tf_op jit(solution)/shard_map/ppermute | solution.py:16
  233.8 5.3 %collective-permute-start.27 = (bf16[128,2048]{1,0:T(8,128)(2,1)S(1)}, bf16[128,2048]{1,0:T(8,128)(2,1)S(1)}, u32[]{:S(2)}, u32[]{:S(2)}) collective-permute-start(bf16[128,2048]{1,0:T(8,128)(2,1)S(1)} %pad_maximum_fusion.11), channel_id=1, source_target_pairs={{0,4},{4,0},{8,12},{12,8},{16,20},{20,16},{24,28},{28,24},{1,5},{5... | collective-permute-start | bytes 1572872 | tf_op jit(solution)/shard_map/ppermute | solution.py:16
  233.9 4.6 %collective-permute-start.28 = (f32[2048]{0:T(1024)S(1)}, f32[2048]{0:T(1024)S(1)}, u32[]{:S(2)}, u32[]{:S(2)}) collective-permute-start(f32[2048]{0:T(1024)S(1)} %copy-done.28), channel_id=1, source_target_pairs={{0,16},{4,20},{8,24},{12,28},{16,0},{20,4},{24,8},{28,12},{1,17},{... | collective-permute-start | bytes 24584 | tf_op jit(solution)/shard_map/ppermute | solution.py:16
  239.5 1.0 copy-start.29
